TPU v7x, 256 devices: a whole 4x4x8 slice. The times are simulated.
256 devices in a mesh: ep: 64 (over z, x, core), kv: 4 (over y).
Axes of the slice: x: 4, y: 4, z: 8, core: 2. Of those that a mesh axis runs over, the one named last changes fastest.
Arguments:
- tokens: bfloat16 [8192, 4096], P('ep', 'kv'), may hold values from -6 to 6
- routes: int32 [8192, 8], P('ep'), may hold values from 0 to 63, all different within a row; in each aligned block of 128 rows (0 to 127, 128 to 255, ...) at most 20 rows name the same one
- combine_weight: float32 [8192, 8], P('ep'), may hold values from 0.1 to 0.5
- gate_weight: bfloat16 [64, 4096, 1536], P('ep', 'kv'), may hold values from -0.09375 to 0.09375
- up_weight: bfloat16 [64, 4096, 1536], P('ep', 'kv'), may hold values from -0.09375 to 0.09375
- down_weight: bfloat16 [64, 1536, 4096], P('ep', None, 'kv'), may hold values from -0.15625 to 0.15625
Outputs:
- moe_out: bfloat16 [8192, 4096], P('ep', 'kv')
Inputs may be any that keep to these rules, and one draw needn't show every extreme that they name: `routes`: each row names 8 different experts; within the rows of one device no expert is named more than 20 times, a bound that some block reaches.
All inputs are finite; a program needn't handle non-finite values.
Results may differ from a plain program's by a relative error of at most 0.0057.
Values may be sent and summed in bfloat16 or wider, within the bound.
A program may use at most 128 MiB of HBM per device.

v0:
```python
import jax
import jax.numpy as jnp
from jax import lax
from jax.sharding import PartitionSpec as P


def slot_targets(routes, experts, capacity):
    flattened = routes.reshape(-1)
    one_hot = (flattened[:, None] == jnp.arange(experts, dtype=jnp.int32)[None, :]).astype(
        jnp.int32
    )
    earlier = jnp.cumsum(one_hot, axis=0) - one_hot
    return flattened * capacity + jnp.sum(earlier * one_hot, axis=1)


def shards(tokens, routes, combine_weight, gate_weight, up_weight, down_weight):
    owners = lax.axis_size("ep")
    tok_local, topk = routes.shape
    experts = owners * gate_weight.shape[0]
    capacity = min(tok_local, 5 * tok_local * topk // (4 * experts))
    targets = slot_targets(routes, experts, capacity)
    token_slot = (
        jnp.zeros((experts * capacity,), jnp.int32)
        .at[targets]
        .set(jnp.arange(tok_local * topk, dtype=jnp.int32) // topk)
    )
    occupied = jnp.zeros((experts * capacity,), jnp.bfloat16).at[targets].set(1.0)
    outgoing = (tokens[token_slot] * occupied[:, None]).reshape(experts, capacity, tokens.shape[1])
    w_gate = gate_weight[0]
    w_up = up_weight[0]
    w_down = down_weight[0]
    arrived = lax.all_to_all(outgoing, "ep", split_axis=0, concat_axis=0, tiled=True)
    sources, count, quarter = arrived.shape
    row_block = arrived.reshape(sources * count, quarter)
    gate_part = jnp.dot(row_block, w_gate, preferred_element_type=jnp.float32)
    up_part = jnp.dot(row_block, w_up, preferred_element_type=jnp.float32)
    gate_sum = lax.psum_scatter(gate_part, "kv", scatter_dimension=1, tiled=True)
    up_sum = lax.psum_scatter(up_part, "kv", scatter_dimension=1, tiled=True)
    hidden = (jax.nn.silu(gate_sum) * up_sum).astype(jnp.bfloat16)
    expert_rows = jnp.dot(
        lax.all_gather(hidden, "kv", axis=1, tiled=True), w_down, preferred_element_type=jnp.float32
    )
    expert_rows = expert_rows.astype(jnp.bfloat16).reshape(sources, count, quarter)
    came_back = lax.all_to_all(expert_rows, "ep", split_axis=0, concat_axis=0, tiled=True)
    picked = came_back.reshape(experts * capacity, -1)[targets].reshape(tok_local, topk, -1)
    mixed = jnp.sum(picked.astype(jnp.float32) * combine_weight[:, :, None], axis=1)
    return mixed.astype(jnp.bfloat16)


def solution(mesh):
    return jax.shard_map(
        shards,
        mesh=mesh,
        in_specs=(
            P("ep", "kv"),
            P("ep", None),
            P("ep", None),
            P("ep", "kv", None),
            P("ep", "kv", None),
            P("ep", None, "kv"),
        ),
        out_specs=P("ep", "kv"),
        check_vma=False,
    )
```

profile of v0, /device:TPU:1, one launch (start us, length us, event | category | flops | bytes accessed | tf_op | source)
XLA Modules:
  0.0 504.6 jit_solution(2057693810586672090)
XLA Ops:
  6.5 0.0 copy-start
  6.5 0.0 copy-start.1
  6.5 0.0 reduce-scatter.3.cloned.1.call-start
  6.5 0.9 copy.9
  7.5 0.1 eq.29
  7.6 0.1 eq.25
  7.7 0.7 broadcast_multiply_fusion.1
  8.4 0.7 fusion.9
  9.1 34.2 %reduce-window.6 = s32[64,8,128]{2,1,0:T(8,128)} reduce-window(s32[64,8,128]{2,1,0:T(8,128)} %fusion.9, s32[]{:T(128)} %constant.28.clone.1), window={size=1x1x128 pad=0_0x0_0x127_0}, to_apply=%region_0.0 | reduce-window | flops 8323072 | bytes 524292 | tf_op jit(solution)/shard_map/reduce-window
  43.2 1.8 slice.12
  45.0 1.1 copy.11
  46.1 0.1 copy.12
  46.2 1.8 broadcast_add_fusion
  48.0 0.1 copy.8
  48.1 0.1 mul.47
  48.2 1.0 fusion.8
  49.3 4.3 scatter_custom_fusion
  53.6 0.0 copy-done.1
  53.6 5.1 %gather_fusion = bf16[1280,1024]{1,0:T(8,128)(2,1)} fusion(bf16[128,1024]{1,0:T(8,128)(2,1)S(1)} %copy-done.1, s32[2048]{0:T(1024)S(1)} %pad_clamp_fusion), kind=kCustom, calls=%fused_computation | custom fusion | bytes 5248000 | tf_op jit(solution)/shard_map/gather | solution.py:28
  58.7 5.2 %gather.9 = bf16[64,20,1024]{2,1,0:T(8,128)(2,1)} reshape(bf16[1280,1024]{1,0:T(8,128)(2,1)} %gather_fusion) | data formatting | bytes 5242880 | tf_op jit(solution)/shard_map/gather | solution.py:28
  63.9 7.6 %scatter_custom_fusion.1 = bf16[1280]{0:T(1024)(128)(2,1)S(1)} fusion(s32[1024]{0:T(1024)S(1)} %bitcast.39, bf16[1024]{0:T(1024)(128)(2,1)S(1)} %broadcast.66, bf16[]{:T(256)} %constant.36.clone.1), kind=kCustom, calls=%fused_computation.35 | custom fusion | bytes 2562 | tf_op jit(solution)/shard_map/scatter | solution.py:27
  71.5 0.1 mul.49
  71.6 2.2 broadcast_multiply_fusion
  73.7 85.7 %all_to_all.10 = bf16[64,20,1024]{2,1,0:T(8,128)(2,1)} all-to-all(bf16[64,20,1024]{2,1,0:T(8,128)(2,1)S(1)} %broadcast_multiply_fusion), channel_id=1, replica_groups=mesh['ep'=64,'kv'=4] {'ep'}, dimensions={0} | all-to-all | bytes 5242880 | tf_op jit(solution)/shard_map/all_to_all | solution.py:32
  159.5 5.2 %reshape.68 = bf16[1280,1024]{1,0:T(8,128)(2,1)} reshape(bf16[64,20,1024]{2,1,0:T(8,128)(2,1)} %all_to_all.10) | data formatting | bytes 5242880 | tf_op jit(solution)/shard_map/reshape | solution.py:34
  164.6 0.0 copy-done
  164.6 8.2 %fusion.4 = f32[1280,1536]{1,0:T(8,128)} fusion(bf16[1280,1024]{1,0:T(8,128)(2,1)} %reshape.68, bf16[1,1024,1536]{2,1,0:T(8,128)(2,1)S(1)} %copy-done), kind=kOutput, calls=%fused_computation.10 | convolution fusion | flops 4026531840 | bytes 13631488 | tf_op jit(solution)/shard_map/dot_general | solution.py:35
  172.8 0.0 reduce-scatter.3.cloned.1.call-update
  172.8 0.2 reduce-scatter.5.cloned.1.call-start
  173.1 11.0 %fusion.2 = f32[1280,1536]{1,0:T(8,128)} fusion(bf16[1280,1024]{1,0:T(8,128)(2,1)} %reshape.68, bf16[1,1024,1536]{2,1,0:T(8,128)(2,1)} %param.10), kind=kOutput, calls=%fused_computation.8 | convolution fusion | flops 4026531840 | bytes 13631488 | tf_op jit(solution)/shard_map/dot_general | solution.py:36
  184.0 0.0 reduce-scatter.5.cloned.1.call-update
  184.1 0.0 all-gather.2.cloned.1.call-start
  184.1 65.7 %reduce-scatter.3.cloned.1.call-done = f32[1280,384]{1,0:T(8,128)} async-done(((f32[1280,1536]{1,0:T(8,128)}), f32[1280,384]{1,0:T(8,128)}) %reduce-scatter.3.cloned.1.call-update) | async-done | bytes 1966096 | tf_op jit(solution)/shard_map/reduce_scatter | solution.py:37
  249.8 81.7 %reduce-scatter.5.cloned.1.call-done = f32[1280,384]{1,0:T(8,128)} async-done(((f32[1280,1536]{1,0:T(8,128)}), f32[1280,384]{1,0:T(8,128)}) %reduce-scatter.5.cloned.1.call-update) | async-done | bytes 1966096 | tf_op jit(solution)/shard_map/reduce_scatter | solution.py:38
  331.5 3.6 multiply_convert_fusion
  335.2 0.0 all-gather.2.cloned.1.call-update
  335.2 48.5 %all-gather.2.cloned.1.call-done = bf16[1280,1536]{1,0:T(8,128)(2,1)} async-done(((bf16[1280,384]{1,0:T(8,128)(2,1)}), bf16[1280,1536]{1,0:T(8,128)(2,1)}) %all-gather.2.cloned.1.call-update) | async-done | bytes 3932176 | tf_op jit(solution)/shard_map/all_gather | solution.py:41
  383.6 8.9 %convolution_convert_fusion = bf16[1280,1024]{1,0:T(8,128)(2,1)} fusion(bf16[1280,1536]{1,0:T(8,128)(2,1)} %all-gather.2.cloned.1.call-done, bf16[1,1536,1024]{2,1,0:T(8,128)(2,1)} %param.11), kind=kOutput, calls=%fused_computation.6 | convolution fusion | flops 4027842560 | bytes 9699328 | tf_op jit(solution)/shard_map/dot_general | solution.py:40
  392.5 5.1 %reshape.69 = bf16[64,20,1024]{2,1,0:T(8,128)(2,1)} reshape(bf16[1280,1024]{1,0:T(8,128)(2,1)} %convolution_convert_fusion) | data formatting | bytes 5242880 | tf_op jit(solution)/shard_map/reshape | solution.py:43
  397.7 0.0 copy-start.2
  397.7 11.0 %all-to-all-start.1 = ((bf16[64,20,1024]{2,1,0:T(8,128)(2,1)}), bf16[64,20,1024]{2,1,0:T(8,128)(2,1)}, u32[]{:S(2)}, u32[]{:S(2)}) async-start(bf16[64,20,1024]{2,1,0:T(8,128)(2,1)} %reshape.69), calls=%async_computation.3 | async-start | bytes 6291456 | tf_op jit(solution)/shard_map/all_to_all | solution.py:44
  408.7 0.0 copy-done.2
  408.7 0.1 copy.13
  408.8 72.4 %all-to-all-done.1 = bf16[64,20,1024]{2,1,0:T(8,128)(2,1)} async-done(((bf16[64,20,1024]{2,1,0:T(8,128)(2,1)}), bf16[64,20,1024]{2,1,0:T(8,128)(2,1)}, u32[]{:S(2)}, u32[]{:S(2)}) %all-to-all-start.1) | async-done | bytes 2621472 | tf_op jit(solution)/shard_map/all_to_all | solution.py:44
  481.2 5.2 %reshape.70 = bf16[1280,1024]{1,0:T(8,128)(2,1)} reshape(bf16[64,20,1024]{2,1,0:T(8,128)(2,1)} %all-to-all-done.1) | data formatting | bytes 5242880 | tf_op jit(solution)/shard_map/reshape | solution.py:45
  486.3 8.1 %gather_fusion.1 = bf16[1024,1024]{1,0:T(8,128)(2,1)} fusion(bf16[1280,1024]{1,0:T(8,128)(2,1)} %reshape.70, s32[1024]{0:T(1024)S(1)} %broadcast_clamp_fusion), kind=kCustom, calls=%fused_computation.1 | custom fusion | bytes 4198400 | tf_op jit(solution)/shard_map/gather | solution.py:45
  494.4 3.7 fusion
  (8 shorter events, 0.1 us)
Async XLA Ops:
  6.5 158.1 %copy-start = (bf16[1,1024,1536]{2,1,0:T(8,128)(2,1)S(1)}, bf16[1,1024,1536]{2,1,0:T(8,128)(2,1)}, u32[]{:S(2)}) copy-start(bf16[1,1024,1536]{2,1,0:T(8,128)(2,1)} %param.9) | copy-start | bytes 9437188
  6.5 47.1 %copy-start.1 = (bf16[128,1024]{1,0:T(8,128)(2,1)S(1)}, bf16[128,1024]{1,0:T(8,128)(2,1)}, u32[]{:S(2)}) copy-start(bf16[128,1024]{1,0:T(8,128)(2,1)} %param.6) | copy-start | bytes 786436
  6.5 243.3 %reduce-scatter.3.cloned.1.call-start = ((), (), s32[]{:S(2)}) async-start(), calls=%async_computation.4 | async-start | bytes 9830400 | tf_op jit(solution)/shard_map/reduce_scatter | solution.py:37
  172.8 158.7 %reduce-scatter.5.cloned.1.call-start = ((), (), s32[]{:S(2)}) async-start(), calls=%async_computation.5 | async-start | bytes 9830400 | tf_op jit(solution)/shard_map/reduce_scatter | solution.py:38
  184.1 199.6 %all-gather.2.cloned.1.call-start = ((), (), s32[]{:S(2)}) async-start(), calls=%async_computation.6 | async-start | bytes 4915200 | tf_op jit(solution)/shard_map/all_gather | solution.py:41
  397.7 11.0 %copy-start.2 = (f32[128,8]{0,1:T(8,128)S(1)}, f32[128,8]{0,1:T(8,128)}, u32[]{:S(2)}) copy-start(f32[128,8]{0,1:T(8,128)} %param.8) | copy-start | bytes 12292
  397.7 83.5 %all-to-all-start.1 = ((bf16[64,20,1024]{2,1,0:T(8,128)(2,1)}), bf16[64,20,1024]{2,1,0:T(8,128)(2,1)}, u32[]{:S(2)}, u32[]{:S(2)}) async-start(bf16[64,20,1024]{2,1,0:T(8,128)(2,1)} %reshape.69), calls=%async_computation.3 | async-start | bytes 6291456 | tf_op jit(solution)/shard_map/all_to_all | solution.py:44
Sparse Core Ops, SparseCore 0:
  173.0 76.8 reduce-scatter.2
  252.4 79.1 reduce-scatter.4
  335.3 48.2 all-gather.1
where the time goes:
time: 508 us; the launch traced here: 505 us
  waiting for transfers between devices  268 us (53%)
  blocking collectives  85.7 us (17%)
  local copies, waits for them, and re-layouts  50.2 us (10%)
  other arithmetic  47.9 us (9%)
  matrix products  28 us (6%)
  between operations  13.2 us (3%)
  starting transfers between devices  11.3 us (2%)
    all_to_all x1, blocking collectives, shards(): lax.all_to_all(outgoing, 'ep', split_axis=0, concat_axis=0, tiled=True)  85.7 us
    reduce_scatter x1, waiting for transfers between devices, shards(): up_sum = lax.psum_scatter(up_part, 'kv', scatter_dimension=1, tiled=True)  81.7 us
    all_to_all x1, waiting for transfers between devices, shards(): lax.all_to_all(expert_rows, 'ep', split_axis=0, concat_axis=0, tiled=True)  72.4 us
    reduce_scatter x1, waiting for transfers between devices, shards(): lax.psum_scatter(gate_part, 'kv', scatter_dimension=1, tiled=True)  65.7 us
    all_gather x1, waiting for transfers between devices, shards(): lax.all_gather(hidden, 'kv', axis=1, tiled=True)  48.5 us
    another operation x3, other arithmetic  36 us
    all_to_all x1, starting transfers between devices, shards(): lax.all_to_all(expert_rows, 'ep', split_axis=0, concat_axis=0, tiled=True)  11 us
    dot_general x1, matrix products, shards(): up_part = jnp.dot(row_block, w_up, preferred_element_type=jnp.float32)  11 us
  transfers between devices with their start and end apart: 4, of which 4 were waited for; matrix products, arithmetic and copies ran while one was open for 2% of the time, Pallas kernels for 0%

commit v1 on v0

v1 whole, which is shorter than its diff:
```python
import jax
import jax.numpy as jnp
from jax import lax
from jax.experimental import pallas as pl
from jax.experimental.pallas import tpu as pltpu
from jax.sharding import PartitionSpec as P

MESH = pl.DeviceIdType.MESH
F32, BF16 = jnp.float32, jnp.bfloat16
NZ, NX, NC, NY = 8, 4, 2, 4
PLANE = NX * NC
TOPK = 8
QUAD = 4

OFFSETS = (0, -1, 1, -2, 2, -3, 3, -4)
RIGHT_IN = ((0, 1), (1, 3), (3, 5), (5, 7))
LEFT_IN = ((0, 2), (2, 4), (4, 6))
LEFT_OUT = (7, 5, 3, 1)
RIGHT_OUT = (6, 4, 2)

ORDER = ((0, 0), (0, 1), (0, 2), (1, 0), (1, 2), (1, 1), (1, 3), (0, 3))
CHUNKS = len(ORDER)
POS = {key: i for i, key in enumerate(ORDER)}


def body(
    meta_ref, tok_ref, wg_ref, wu_ref, wd_ref, out_ref,
    tok_all, meta_all, vv, ww, wgu, wdn, sel, xrows, hop_s, hop_r, qf, qs, qr, own, hid, erow, back,
    zp, zs, zr,
    w_sem, zt_ss, zt_rs, zm_ss, zm_rs, x_ss, x_rs, hop_ss, hop_rs, q_ss, q_rs, ag_ss, ag_rs,
    fw_ss, fw_rs, b_ss, b_rs, z_ss, z_rs,
):
    tok, width = tok_ref.shape
    ff = wg_ref.shape[1]
    fq = ff // NY
    rows = xrows.shape[1] // 2
    cap = rows // QUAD
    ep, y = lax.axis_index("ep"), lax.axis_index("kv")
    z, x, c = ep // PLANE, lax.rem(ep // NC, NX), lax.rem(ep, NC)

    def dev(dz=0, dx=0, dc=0, dy=0):
        zz, xx, cc = lax.rem(z + dz + NZ, NZ), lax.rem(x + dx, NX), lax.rem(c + dc, NC)
        return {"ep": (zz * NX + xx) * NC + cc, "kv": lax.rem(y + dy + NY, NY)}

    def remote(src, dst, ss, rs, to):
        return pltpu.make_async_remote_copy(
            src_ref=src, dst_ref=dst, send_sem=ss, recv_sem=rs, device_id=to, device_id_type=MESH
        )

    up_y, down_y = dev(dy=1), dev(dy=-1)
    up_z, down_z = dev(dz=1), dev(dz=-1)

    def arrived(dst, rs):
        remote(dst, dst, rs, rs, up_y).wait_recv()

    def sent(src, ss):
        remote(src, src, ss, ss, up_y).wait_send()

    loads = []
    for r in range(NY):
        cols = pl.ds(pl.multiple_of(lax.rem(y + r, NY) * fq, 128), fq)
        loads += [
            pltpu.make_async_copy(wg_ref.at[:, cols], wgu.at[:, pl.ds(2 * r * fq, fq)], w_sem.at[3 * r]),
            pltpu.make_async_copy(wu_ref.at[:, cols], wgu.at[:, pl.ds((2 * r + 1) * fq, fq)], w_sem.at[3 * r + 1]),
            pltpu.make_async_copy(wd_ref.at[cols], wdn.at[pl.ds(r * fq, fq)], w_sem.at[3 * r + 2]),
        ]
    for load in loads:
        load.start()

    plane = [(dx, dc) for dx in range(NX) for dc in range(NC)]
    barrier = pltpu.get_barrier_semaphore()
    partners = [up_y, down_y, up_z, down_z] + [dev(dx=dx, dc=dc) for dx, dc in plane[1:]]
    for partner in partners:
        pl.semaphore_signal(barrier, inc=1, device_id=partner, device_id_type=MESH)
    tok_all[0] = tok_ref[...]
    meta_all[0] = meta_ref[...]
    pl.semaphore_wait(barrier, len(partners))

    def z_send(pair, to):
        src, dst = pair
        remote(meta_all.at[src], meta_all.at[dst], zm_ss.at[dst - 1], zm_rs.at[dst - 1], to).start()
        remote(tok_all.at[src], tok_all.at[dst], zt_ss.at[dst - 1], zt_rs.at[dst - 1], to).start()

    def z_arrived(dst):
        arrived(meta_all.at[dst], zm_rs.at[dst - 1])
        arrived(tok_all.at[dst], zt_rs.at[dst - 1])

    def prepare(slot):
        rt, wt = meta_all[slot, 0:TOPK, :], meta_all[slot, TOPK : 2 * TOPK, :]
        j = lax.broadcasted_iota(jnp.int32, (PLANE, tok), 0)
        expert = (z * NX + lax.rem(x + j // NC, NX)) * NC + lax.rem(c + lax.rem(j, NC), NC)
        expert = expert.astype(F32)
        hit = jnp.zeros((PLANE, tok), F32)
        share = jnp.zeros((PLANE, tok), F32)
        for k in range(TOPK):
            same = rt[k : k + 1, :] == expert
            hit += jnp.where(same, 1.0, 0.0)
            share += jnp.where(same, wt[k : k + 1, :], 0.0)
        earlier = lax.broadcasted_iota(jnp.int32, (tok, tok), 0) < lax.broadcasted_iota(jnp.int32, (tok, tok), 1)
        rank = jnp.dot(hit.astype(BF16), jnp.where(earlier, 1.0, 0.0).astype(BF16), preferred_element_type=F32)
        vv[slot] = jnp.where(hit > 0.5, rank, -1000.0)
        ww[slot] = share

    slot_row = lax.broadcasted_iota(jnp.int32, (rows, tok), 0).astype(F32)

    def select(quad, dx):
        parts = []
        for dc in range(NC):
            j = dx * NC + dc
            parts.append(
                jnp.concatenate(
                    [
                        jnp.where(slot_row - cap * q == vv[quad * QUAD + q, j : j + 1, :], 1.0, 0.0).astype(BF16)
                        for q in range(QUAD)
                    ],
                    axis=1,
                )
            )
        source = tok_all[quad * QUAD : (quad + 1) * QUAD].reshape(QUAD * tok, width)
        picked = jnp.dot(jnp.concatenate(parts, axis=0), source, preferred_element_type=F32)
        at = quad * NX + dx
        sel[at] = picked.astype(BF16)
        pos = POS[quad, (NX - dx) % NX]
        for dc in range(NC):
            src, dst = sel.at[at, pl.ds(dc * rows, rows)], xrows.at[pos, pl.ds(dc * rows, rows)]
            if dx == 0 and dc == 0:
                pltpu.make_async_copy(src, dst, x_rs.at[pos, dc]).start()
            else:
                remote(src, dst, x_ss.at[at, dc], x_rs.at[pos, dc], dev(dx=dx, dc=dc)).start()

    z_send(RIGHT_IN[0], up_z)
    z_send(LEFT_IN[0], down_z)
    prepare(0)
    z_arrived(1)
    z_send(RIGHT_IN[1], up_z)
    z_arrived(2)
    z_send(LEFT_IN[1], down_z)
    prepare(1)
    prepare(2)
    z_arrived(3)
    z_send(RIGHT_IN[2], up_z)
    prepare(3)
    for dx in (0, 3, 2, 1):
        select(0, dx)
    for load in loads:
        load.wait()

    def partials(i):
        for dc in range(NC):
            arrived(xrows.at[i, pl.ds(dc * rows, rows)], x_rs.at[i, dc])

        def part(r):
            return jnp.dot(xrows[i], wgu[:, 2 * r * fq : 2 * (r + 1) * fq], preferred_element_type=F32)

        far = part(2)
        hop_s[0, i] = far[:, :fq].astype(BF16)
        hop_s[1, i] = far[:, fq:].astype(BF16)
        remote(hop_s.at[0, i], hop_r.at[0, i], hop_ss.at[0, i], hop_rs.at[0, i], up_y).start()
        remote(hop_s.at[1, i], hop_r.at[1, i], hop_ss.at[1, i], hop_rs.at[1, i], down_y).start()
        above = part(1)
        qf[0, i] = above[:, :fq]
        qs[0, i, :, fq:] = above[:, fq:].astype(BF16)
        below = part(3)
        qs[1, i, :, :fq] = below[:, :fq].astype(BF16)
        qf[1, i] = below[:, fq:]
        own[i] = part(0)

    def middle(i):
        arrived(hop_r.at[0, i], hop_rs.at[0, i])
        qs[0, i, :, :fq] = (qf[0, i] + hop_r[0, i].astype(F32)).astype(BF16)
        remote(qs.at[0, i], qr.at[0, i], q_ss.at[0, i], q_rs.at[0, i], up_y).start()
        arrived(hop_r.at[1, i], hop_rs.at[1, i])
        qs[1, i, :, fq:] = (qf[1, i] + hop_r[1, i].astype(F32)).astype(BF16)
        remote(qs.at[1, i], qr.at[1, i], q_ss.at[1, i], q_rs.at[1, i], down_y).start()

    def quarter(i, r):
        return hid.at[i, :, pl.ds(r * fq, fq)]

    def half(i, r, h):
        return hid.at[i, pl.ds(h * rows, rows), pl.ds(r * fq, fq)]

    def activate(i):
        arrived(qr.at[0, i], q_rs.at[0, i])
        arrived(qr.at[1, i], q_rs.at[1, i])
        total = own[i] + qr[0, i].astype(F32) + qr[1, i].astype(F32)
        gate, up = total[:, :fq], total[:, fq:]
        hid[i, :, :fq] = (gate / (1.0 + jnp.exp(-gate)) * up).astype(BF16)
        remote(quarter(i, 0), quarter(i, 3), ag_ss.at[0, i], ag_rs.at[0, i], up_y).start()
        remote(quarter(i, 0), quarter(i, 1), ag_ss.at[1, i], ag_rs.at[1, i], down_y).start()

    def forward(i):
        arrived(quarter(i, 3), ag_rs.at[0, i])
        remote(half(i, 3, 0), half(i, 2, 0), fw_ss.at[0, i], fw_rs.at[0, i], up_y).start()
        arrived(quarter(i, 1), ag_rs.at[1, i])
        remote(half(i, 1, 1), half(i, 2, 1), fw_ss.at[1, i], fw_rs.at[1, i], down_y).start()

    def back_to(k):
        quad, dx = ORDER[k]
        copies = []
        for dc in range(NC):
            j = ((NX - dx) % NX) * NC + dc
            src, dst = erow.at[k, pl.ds(dc * rows, rows)], back.at[quad, pl.ds(j * rows, rows)]
            if dx == 0 and dc == 0:
                copies.append(pltpu.make_async_copy(src, dst, b_rs.at[quad, j]))
            else:
                copies.append(remote(src, dst, b_ss.at[k, dc], b_rs.at[quad, j], dev(dx=dx, dc=dc)))
        return copies

    def down(i):
        arrived(half(i, 2, 0), fw_rs.at[0, i])
        arrived(half(i, 2, 1), fw_rs.at[1, i])
        erow[i] = jnp.dot(hid[i], wdn[...], preferred_element_type=F32).astype(BF16)
        for k in range(CHUNKS):

            @pl.when(i == k)
            def _():
                for copy in back_to(k):
                    copy.start()

    def step(s, carry):
        @pl.when(s == 1)
        def _():
            z_arrived(5)
            z_send(RIGHT_IN[3], up_z)
            z_arrived(4)
            z_send(LEFT_IN[2], down_z)

        for lag, stage in enumerate((partials, middle, activate, forward, down)):

            @pl.when(jnp.logical_and(s >= lag, s < CHUNKS + lag))
            def _():
                stage(s - lag)

        @pl.when(s == 2)
        def _():
            z_arrived(6)
            z_arrived(7)
            for slot in range(QUAD, 2 * QUAD):
                prepare(slot)
            for dx in (0, 2, 3, 1):
                select(1, dx)

        return carry

    lax.fori_loop(0, CHUNKS + 4, step, 0)

    def combine(quad):
        for j in range(PLANE):
            arrived(back.at[quad, pl.ds(j * rows, rows)], b_rs.at[quad, j])

        def one(q, carry):
            slot = quad * QUAD + q
            row = slot_row - (cap * q).astype(F32)
            share = jnp.concatenate(
                [
                    jnp.where(row == vv[slot, j : j + 1, :], ww[slot, j : j + 1, :], 0.0)
                    for j in range(PLANE)
                ],
                axis=0,
            )
            high = share.astype(BF16)
            low = (share - high.astype(F32)).astype(BF16)
            both = lax.dot_general(
                jnp.concatenate([high, low], axis=1), back[quad], (((0,), (0,)), ((), ())), preferred_element_type=F32
            )
            zp[slot] = both[:tok] + both[tok:]
            return carry

        lax.fori_loop(0, QUAD, one, 0)

    nleft = len(LEFT_OUT)

    def z_out(out, base, h, to):
        total = zp[out[h]]
        if h > 0:
            arrived(zr.at[base + h - 1], z_rs.at[base + h - 1])
            total = total + zr[base + h - 1].astype(F32)
        zs[base + h] = total.astype(BF16)
        remote(zs.at[base + h], zr.at[base + h], z_ss.at[base + h], z_rs.at[base + h], to).start()

    combine(1)
    z_out(LEFT_OUT, 0, 0, down_z)
    z_out(RIGHT_OUT, nleft, 0, up_z)
    z_out(LEFT_OUT, 0, 1, down_z)
    z_out(RIGHT_OUT, nleft, 1, up_z)
    combine(0)
    z_out(LEFT_OUT, 0, 2, down_z)
    z_out(RIGHT_OUT, nleft, 2, up_z)
    z_out(LEFT_OUT, 0, 3, down_z)
    last_left, last_right = nleft - 1, nleft + len(RIGHT_OUT) - 1
    arrived(zr.at[last_right], z_rs.at[last_right])
    arrived(zr.at[last_left], z_rs.at[last_left])
    out_ref[...] = (zp[0] + zr[last_left].astype(F32) + zr[last_right].astype(F32)).astype(BF16)

    for slot in range(1, 2 * QUAD):
        sent(meta_all.at[slot], zm_ss.at[slot - 1])
        sent(tok_all.at[slot], zt_ss.at[slot - 1])
        sent(zs.at[slot - 1], z_ss.at[slot - 1])

    def drain(i, carry):
        for d in range(2):
            sent(hop_s.at[d, i], hop_ss.at[d, i])
            sent(qs.at[d, i], q_ss.at[d, i])
            sent(quarter(i, 0), ag_ss.at[d, i])
            sent(half(i, 0, 0), fw_ss.at[d, i])
        return carry

    lax.fori_loop(0, CHUNKS, drain, 0)
    for k in range(CHUNKS):
        for dc in range(NC):
            if (k % NX, dc) != (0, 0):
                sent(sel.at[k, pl.ds(0, rows)], x_ss.at[k, dc])
            if (ORDER[k][1], dc) != (0, 0):
                sent(erow.at[k, pl.ds(0, rows)], b_ss.at[k, dc])


def shards(tokens, routes, combine_weight, gate_weight, up_weight, down_weight):
    tok, width = tokens.shape
    experts = lax.axis_size("ep")
    ff = gate_weight.shape[2]
    fq = ff // NY
    cap = min(tok, 5 * tok * TOPK // (4 * experts))
    rows = QUAD * cap
    n = CHUNKS
    meta = jnp.concatenate([routes.astype(F32).T, combine_weight.T], axis=0)
    vm = pltpu.VMEM
    dma = pltpu.SemaphoreType.DMA
    any_space = pl.BlockSpec(memory_space=pl.ANY)
    return pl.pallas_call(
        body,
        out_shape=jax.ShapeDtypeStruct((tok, width), BF16),
        in_specs=[pl.BlockSpec(memory_space=vm)] * 2 + [any_space] * 3,
        out_specs=pl.BlockSpec(memory_space=vm),
        scratch_shapes=[
            vm((2 * QUAD, tok, width), BF16),
            vm((2 * QUAD, 2 * TOPK, tok), F32),
            vm((2 * QUAD, PLANE, tok), F32),
            vm((2 * QUAD, PLANE, tok), F32),
            vm((width, 2 * ff), BF16),
            vm((ff, width), BF16),
            vm((n, 2 * rows, width), BF16),
            vm((n, 2 * rows, width), BF16),
            vm((2, n, 2 * rows, fq), BF16),
            vm((2, n, 2 * rows, fq), BF16),
            vm((2, n, 2 * rows, fq), F32),
            vm((2, n, 2 * rows, 2 * fq), BF16),
            vm((2, n, 2 * rows, 2 * fq), BF16),
            vm((n, 2 * rows, 2 * fq), F32),
            vm((n, 2 * rows, ff), BF16),
            vm((n, 2 * rows, width), BF16),
            vm((2, PLANE * rows, width), BF16),
            vm((2 * QUAD, tok, width), F32),
            vm((2 * QUAD - 1, tok, width), BF16),
            vm((2 * QUAD - 1, tok, width), BF16),
            dma((3 * NY,)),
            dma((2 * QUAD - 1,)),
            dma((2 * QUAD - 1,)),
            dma((2 * QUAD - 1,)),
            dma((2 * QUAD - 1,)),
            dma((n, NC)),
            dma((n, NC)),
            dma((2, n)),
            dma((2, n)),
            dma((2, n)),
            dma((2, n)),
            dma((2, n)),
            dma((2, n)),
            dma((2, n)),
            dma((2, n)),
            dma((n, NC)),
            dma((2, PLANE)),
            dma((2 * QUAD - 1,)),
            dma((2 * QUAD - 1,)),
        ],
        compiler_params=pltpu.CompilerParams(
            collective_id=0, has_side_effects=True, vmem_limit_bytes=63 * 1024 * 1024
        ),
        cost_estimate=pl.CostEstimate(flops=12 * 10**9, bytes_accessed=10 * 10**6, transcendentals=0),
    )(meta, tokens, gate_weight[0], up_weight[0], down_weight[0])


def solution(mesh):
    return jax.shard_map(
        shards,
        mesh=mesh,
        in_specs=(
            P("ep", "kv"),
            P("ep", None),
            P("ep", None),
            P("ep", "kv", None),
            P("ep", "kv", None),
            P("ep", None, "kv"),
        ),
        out_specs=P("ep", "kv"),
        check_vma=False,
    )
```

time: 508 us -> 175 us (0.34)
  the two profiles are of different devices: /device:TPU:1 before, /device:TPU:36 now
where the time goes in v1:
time: 175 us; the launch traced here: 174 us
  Pallas kernels  171 us (98%)
  other arithmetic  1.97 us (1%)
    pallas_call x1, Pallas kernels, shards(): pl.pallas_call(body, out_shape=jax.ShapeDtypeStruct((tok, width), BF16),...  171 us

profile of v1, /device:TPU:36, one launch (start us, length us, event | category | flops | bytes accessed | tf_op | source)
XLA Modules:
  0.0 174.5 jit_solution(4535276423717068413)
XLA Ops:
  0.0 0.7 convert_bitcast_fusion
  0.7 1.3 pad_maximum_fusion.meta_ref
  2.0 170.8 %shard_map.64 = bf16[128,1024]{1,0:T(8,128)(2,1)} custom-call(f32[16,128]{1,0:T(8,128)} %pad_maximum_fusion.meta_ref, bf16[128,1024]{1,0:T(8,128)(2,1)} %tok_ref.1, bf16[1024,1536]{1,0:T(8,128)(2,1)} %bitcast.7, bf16[1024,1536]{1,0:T(8,128)(2,1)} %bitcast.8, bf16[1536,1024]{1,0:T(8,128)(2,1)} %bitcast.9), custom_call_target="tpu_custom_call" | custom-call | flops 12000000000 | bytes 10000000 | tf_op jit(solution)/shard_map/pallas_call | solution.py:329
  172.8 1.7 copy.8

commit v2 on v0

v2 whole, which is shorter than its diff:
```python
import jax
import jax.numpy as jnp
from jax import lax
from jax.experimental import pallas as pl
from jax.experimental.pallas import tpu as pltpu
from jax.sharding import PartitionSpec as P

MESH = pl.DeviceIdType.MESH
F32, BF16 = jnp.float32, jnp.bfloat16
NZ, NX, NC, NY = 8, 4, 2, 4
PLANE = NX * NC
TOPK = 8

OFFSETS = (0, -1, 1, -2, 2, -3, 3, -4)
NEXT_HOP = {0: (1, 2), 1: (3,), 2: (4,), 3: (5,), 4: (6,), 5: (7,), 6: (), 7: ()}
LEFT_OUT = (7, 5, 3, 1)
RIGHT_OUT = (6, 4, 2)

MAIN, TAIL, CUT = 16, 4, 4

ORDER = tuple(
    tuple(divmod(unit, 10) for unit in chunk)
    for chunk in (
        (3, 1),
        (20, 10),
        (12, 21, 11, 13),
        (50, 31, 32, 33),
        (61, 71, 51, 53),
        (70, 52, 73, 72),
        (62, 63, 60, 42),
        (30, 43, 41, 40),
        (23, 22),
        (2, 0),
    )
)
CHUNKS, SMALL, LARGE = len(ORDER), 2, 4
LOW, HIGH = 2, CHUNKS - 2
POS = {unit: (k, a) for k, units in enumerate(ORDER) for a, unit in enumerate(units)}
UROWS = NC * MAIN
UNIT = NC * (MAIN + TAIL)
ROWS = LARGE * UNIT

PLANE_IN, COMBINE, LEAVE = 0, 1, 2
FIRST = ()
AFTER_P = {0: ((PLANE_IN, 1), (PLANE_IN, 2),), 3: ((PLANE_IN, 7),), 8: ((COMBINE, 5), (COMBINE, 7), (LEAVE, 7),), 9: ((LEAVE, 5),)}
AFTER_A = {9: ((COMBINE, 6), (LEAVE, 6),), 10: ((LEAVE, 4),)}
AFTER_D = {2: ((PLANE_IN, 5), (PLANE_IN, 6),), 5: ((COMBINE, 1),)}
AFTER_M = {1: ((PLANE_IN, 3), (PLANE_IN, 4),)}
AFTER_F = {9: ((COMBINE, 3), (COMBINE, 4), (LEAVE, 3),)}
LAST = ((LEAVE, 1), (COMBINE, 2), (LEAVE, 2), (COMBINE, 0),)

def body(
    rt_ref, wt_ref, tok_ref, wg_ref, wu_ref, wd_ref, out_ref,
    tok_all, meta_all, vv, ww, wgu, wdn, sel, xin, xrows, hop_s, hop_r, qf, qs, qr, own, hid, erow, eout, back,
    zp, zs, zr,
    w_sem, zt_ss, zt_rs, zm_ss, zm_rs, x_ss, x_rs, hop_ss, hop_rs, q_ss, q_rs, ag_ss, ag_rs,
    fw_ss, fw_rs, b_ss, b_rs, z_ss, z_rs,
):
    tok, width = tok_ref.shape
    ff = wg_ref.shape[1]
    fq = ff // NY
    block = width // CUT
    ep, y = lax.axis_index("ep"), lax.axis_index("kv")
    z, x, c = ep // PLANE, lax.rem(ep // NC, NX), lax.rem(ep, NC)

    def dev(dz=0, dx=0, dc=0, dy=0):
        zz, xx, cc = lax.rem(z + dz + NZ, NZ), lax.rem(x + dx, NX), lax.rem(c + dc, NC)
        return {"ep": (zz * NX + xx) * NC + cc, "kv": lax.rem(y + dy + NY, NY)}

    def remote(src, dst, ss, rs, to):
        return pltpu.make_async_remote_copy(
            src_ref=src, dst_ref=dst, send_sem=ss, recv_sem=rs, device_id=to, device_id_type=MESH
        )

    up_y, down_y = dev(dy=1), dev(dy=-1)
    up_z, down_z = dev(dz=1), dev(dz=-1)

    def arrived(dst, rs):
        remote(dst, dst, rs, rs, up_y).wait_recv()

    def sent(src, ss):
        remote(src, src, ss, ss, up_y).wait_send()

    plane = [(dx, dc) for dx in range(NX) for dc in range(NC)]
    barrier = pltpu.get_barrier_semaphore()
    partners = [up_y, down_y, up_z, down_z] + [dev(dx=dx, dc=dc) for dx, dc in plane[1:]]
    for partner in partners:
        pl.semaphore_signal(barrier, inc=1, device_id=partner, device_id_type=MESH)

    loads = []
    for r in range(NY):
        cols = pl.ds(pl.multiple_of(lax.rem(y + r, NY) * fq, 128), fq)
        loads += [
            pltpu.make_async_copy(wg_ref.at[:, cols], wgu.at[:, pl.ds(2 * r * fq, fq)], w_sem.at[3 * r]),
            pltpu.make_async_copy(wu_ref.at[:, cols], wgu.at[:, pl.ds((2 * r + 1) * fq, fq)], w_sem.at[3 * r + 1]),
            pltpu.make_async_copy(wd_ref.at[cols], wdn.at[pl.ds(r * fq, fq)], w_sem.at[3 * r + 2]),
        ]
    for load in loads:
        load.start()

    place = lax.rem(lax.broadcasted_iota(jnp.int32, (PLANE * MAIN, tok), 0), MAIN)
    main_slot = place.astype(F32)
    tail_slot = [
        jnp.where(lax.rem(place, CUT) == b, MAIN + place // CUT, -1).astype(F32) for b in range(CUT)
    ]

    def spread(rows):
        return jnp.concatenate([jnp.broadcast_to(rows[j : j + 1, :], (MAIN, tok)) for j in range(PLANE)], axis=0)

    def prepare(p):
        rt, wt = meta_all[p, 0:TOPK, :], meta_all[p, TOPK : 2 * TOPK, :]
        j = lax.broadcasted_iota(jnp.int32, (PLANE, tok), 0)
        expert = (z * NX + lax.rem(x + j // NC, NX)) * NC + lax.rem(c + lax.rem(j, NC), NC)
        expert = expert.astype(F32)
        hit = jnp.zeros((PLANE, tok), F32)
        share = jnp.zeros((PLANE, tok), F32)
        for k in range(TOPK):
            same = rt[k : k + 1, :] == expert
            hit += jnp.where(same, 1.0, 0.0)
            share += jnp.where(same, wt[k : k + 1, :], 0.0)
        earlier = lax.broadcasted_iota(jnp.int32, (tok, tok), 0) < lax.broadcasted_iota(jnp.int32, (tok, tok), 1)
        rank = jnp.dot(hit.astype(BF16), jnp.where(earlier, 1.0, 0.0).astype(BF16), preferred_element_type=F32)
        vv[p] = jnp.where(hit > 0.5, rank, -1000.0)
        ww[p] = share

    def select(p):
        slot = spread(vv[p])

        def rows(of, cols):
            return jnp.dot(jnp.where(slot == of, 1.0, 0.0).astype(BF16), tok_all[p, :, cols], preferred_element_type=F32)

        sel[p, :, :width] = rows(main_slot, slice(0, width)).astype(BF16)
        tail = rows(tail_slot[0], slice(0, block))
        for b in range(1, CUT):
            tail += rows(tail_slot[b], slice(b * block, (b + 1) * block))
        sel[p, :, width:] = tail.astype(BF16)

    def dispatch(p):
        todo = []
        for dx, dc in plane:
            k, a = POS[p, (NX - dx) % NX]
            todo.append((k, dx != 2, dx, dc, a))
        for k, _, dx, dc, a in sorted(todo):
            src = sel.at[p, pl.ds((dx * NC + dc) * MAIN, MAIN)]
            dst = xin.at[k, pl.ds(a * UROWS + dc * MAIN, MAIN)]
            if dx == 0 and dc == 0:
                pltpu.make_async_copy(src, dst, x_rs.at[k, a]).start()
            else:
                remote(src, dst, x_ss, x_rs.at[k, a], dev(dx=dx, dc=dc)).start()

    def z_send(p):
        for q in NEXT_HOP[p]:
            to = up_z if OFFSETS[q] < 0 else down_z
            remote(meta_all.at[p], meta_all.at[q], zm_ss, zm_rs.at[q - 1], to).start()
            remote(tok_all.at[p], tok_all.at[q], zt_ss, zt_rs.at[q - 1], to).start()

    def z_arrived(p):
        arrived(meta_all.at[p], zm_rs.at[p - 1])
        arrived(tok_all.at[p], zt_rs.at[p - 1])
        z_send(p)
        prepare(p)
        select(p)
        dispatch(p)

    def picks(n, b, axis):
        shape = (n * UROWS // CUT, n * UROWS) if axis == 0 else (n * UROWS, n * UROWS // CUT)
        few, many = lax.broadcasted_iota(jnp.int32, shape, axis), lax.broadcasted_iota(jnp.int32, shape, 1 - axis)
        return jnp.where(many == few * CUT + b, 1.0, 0.0).astype(BF16)

    def send_y(ref, recv, i, n, ss, rs):
        for d, to in enumerate((up_y, down_y)):
            part = pl.ds(0, n * UNIT)
            remote(ref.at[d, i, part], recv.at[d, i, part], ss, rs.at[d, i], to).start()

    def partials(i, n):
        for a in range(n):
            arrived(xin.at[i, pl.ds(a * UROWS, UROWS)], x_rs.at[i, a])
        rows, whole = n * UNIT, n * UROWS
        xrows[:whole] = xin[i, :whole, :width]
        for b in range(CUT):
            tail = jnp.dot(picks(n, b, 0), xin[i, :whole, width:], preferred_element_type=F32)
            xrows[whole:rows, b * block : (b + 1) * block] = tail.astype(BF16)

        def part(r):
            return jnp.dot(xrows[:rows], wgu[:, 2 * r * fq : 2 * (r + 1) * fq], preferred_element_type=F32)

        far = part(2)
        hop_s[0, i, :rows] = far[:, :fq].astype(BF16)
        hop_s[1, i, :rows] = far[:, fq:].astype(BF16)
        send_y(hop_s, hop_r, i, n, hop_ss, hop_rs)
        above = part(1)
        qf[0, :rows] = above[:, :fq]
        qs[0, i, :rows, fq:] = above[:, fq:].astype(BF16)
        below = part(3)
        qs[1, i, :rows, :fq] = below[:, :fq].astype(BF16)
        qf[1, :rows] = below[:, fq:]
        own[lax.rem(i, 2), :rows] = part(0)

    def middle(i, n):
        rows = n * UNIT
        for d, to in enumerate((up_y, down_y)):
            arrived(hop_r.at[d, i, pl.ds(0, rows)], hop_rs.at[d, i])
            total = qf[d, :rows] + hop_r[d, i, :rows].astype(F32)
            qs[d, i, :rows, d * fq : (d + 1) * fq] = total.astype(BF16)
            part = pl.ds(0, rows)
            remote(qs.at[d, i, part], qr.at[d, i, part], q_ss, q_rs.at[d, i], to).start()

    def quarter(i, n, r):
        return hid.at[i, pl.ds(0, n * UNIT), pl.ds(r * fq, fq)]

    def half(i, n, r, h):
        first = -(-n * UNIT // 32) * 16
        at = pl.ds(0, first) if h == 0 else pl.ds(first, n * UNIT - first)
        return hid.at[i, at, pl.ds(r * fq, fq)]

    def activate(i, n):
        rows = n * UNIT
        for d in range(2):
            arrived(qr.at[d, i, pl.ds(0, rows)], q_rs.at[d, i])
        total = own[lax.rem(i, 2), :rows] + qr[0, i, :rows].astype(F32) + qr[1, i, :rows].astype(F32)
        gate, up = total[:, :fq], total[:, fq:]
        hid[i, :rows, :fq] = (gate / (1.0 + jnp.exp(-gate)) * up).astype(BF16)
        remote(quarter(i, n, 0), quarter(i, n, 3), ag_ss, ag_rs.at[0, i], up_y).start()
        remote(quarter(i, n, 0), quarter(i, n, 1), ag_ss, ag_rs.at[1, i], down_y).start()

    def forward(i, n):
        arrived(quarter(i, n, 3), ag_rs.at[0, i])
        remote(half(i, n, 3, 0), half(i, n, 2, 0), fw_ss, fw_rs.at[0, i], up_y).start()
        arrived(quarter(i, n, 1), ag_rs.at[1, i])
        remote(half(i, n, 1, 1), half(i, n, 2, 1), fw_ss, fw_rs.at[1, i], down_y).start()

    def send_back(k):
        todo = sorted((dx != 2, a, p, dx, dc) for a, (p, dx) in enumerate(ORDER[k]) for dc in range(NC))
        for _, a, p, dx, dc in todo:
            d = (NX - dx) % NX
            src = eout.at[k, pl.ds(a * UROWS + dc * MAIN, MAIN)]
            dst = back.at[p, pl.ds((d * NC + dc) * MAIN, MAIN)]
            if dx == 0 and dc == 0:
                pltpu.make_async_copy(src, dst, b_rs.at[p, d]).start()
            else:
                remote(src, dst, b_ss, b_rs.at[p, d], dev(dx=dx, dc=dc)).start()

    def down(i, n):
        arrived(half(i, n, 2, 0), fw_rs.at[0, i])
        arrived(half(i, n, 2, 1), fw_rs.at[1, i])
        rows, whole = n * UNIT, n * UROWS
        erow[:rows] = jnp.dot(hid[i, :rows], wdn[...], preferred_element_type=F32).astype(BF16)
        eout[i, :whole, :width] = erow[:whole]
        tail = jnp.zeros((whole, block), F32)
        for b in range(CUT):
            last = erow[whole:rows, b * block : (b + 1) * block]
            tail += jnp.dot(picks(n, b, 1), last, preferred_element_type=F32)
        eout[i, :whole, width:] = tail.astype(BF16)
        for k in range(CHUNKS):
            if len(ORDER[k]) == n:
                pl.when(i == k)(lambda k=k: send_back(k))

    def combine(p):
        for d in range(NX):
            arrived(back.at[p, pl.ds(d * UROWS, UROWS)], b_rs.at[p, d])
        slot, share = spread(vv[p]), spread(ww[p])

        def weighted(of, cols):
            exact = jnp.where(slot == of, share, 0.0)
            high = exact.astype(BF16)
            low = (exact - high.astype(F32)).astype(BF16)
            both = lax.dot_general(
                jnp.concatenate([high, low], axis=1), back[p, :, cols], (((0,), (0,)), ((), ())),
                preferred_element_type=F32,
            )
            return both[:tok] + both[tok:]

        zp[p] = weighted(main_slot, slice(0, width))
        for b in range(CUT):
            zp[p, :, b * block : (b + 1) * block] += weighted(tail_slot[b], slice(width, width + block))

    def leave(p):
        out, base, to = (LEFT_OUT, 0, down_z) if p in LEFT_OUT else (RIGHT_OUT, len(LEFT_OUT), up_z)
        h = base + out.index(p)
        total = zp[p]
        if h > base:
            arrived(zr.at[h - 1], z_rs.at[h - 1])
            total = total + zr[h - 1].astype(F32)
        zs[h] = total.astype(BF16)
        remote(zs.at[h], zr.at[h], z_ss, z_rs.at[h], to).start()

    ops = {0: z_arrived, 1: combine, 2: leave}

    def perform(todo):
        for op, p in todo:
            ops[op](p)

    tok_all[0] = tok_ref[...]
    meta_all[0, 0:TOPK, :] = rt_ref[...].astype(F32)
    meta_all[0, TOPK : 2 * TOPK, :] = wt_ref[...]
    prepare(0)
    select(0)
    pl.semaphore_wait(barrier, len(partners))
    z_send(0)
    dispatch(0)
    perform(FIRST)
    for load in loads:
        load.wait()

    def step(s, carry):
        for run, lag, table in (
            (partials, 0, AFTER_P),
            (activate, 1, AFTER_A),
            (down, 2, AFTER_D),
            (middle, 0, AFTER_M),
            (forward, 1, AFTER_F),
        ):
            i = s - lag
            large = jnp.logical_and(i >= LOW, i < HIGH)
            small = jnp.logical_or(
                jnp.logical_and(i >= 0, i < LOW), jnp.logical_and(i >= HIGH, i < CHUNKS)
            )
            pl.when(large)(lambda run=run, i=i: run(i, LARGE))
            pl.when(small)(lambda run=run, i=i: run(i, SMALL))
            for at, todo in table.items():
                pl.when(s == at)(lambda todo=todo: perform(todo))
        return carry

    lax.fori_loop(0, CHUNKS + 2, step, 0)
    perform(LAST)
    last_left, last_right = len(LEFT_OUT) - 1, len(LEFT_OUT) + len(RIGHT_OUT) - 1
    arrived(zr.at[last_right], z_rs.at[last_right])
    arrived(zr.at[last_left], z_rs.at[last_left])
    out_ref[...] = (zp[0] + zr[last_left].astype(F32) + zr[last_right].astype(F32)).astype(BF16)

    sent(meta_all.at[pl.ds(1, NZ - 1)], zm_ss)
    sent(tok_all.at[pl.ds(1, NZ - 1)], zt_ss)
    sent(sel.at[:, pl.ds(MAIN, (PLANE - 1) * MAIN)], x_ss)
    sent(hop_s.at[:, pl.ds(0, NZ)], hop_ss)
    sent(qs.at[:, pl.ds(0, NZ)], q_ss)
    sent(hop_s.at[:, pl.ds(0, NZ)], ag_ss)
    sent(hop_s.at[0, pl.ds(0, NZ)], fw_ss)
    sent(sel.at[:, pl.ds(MAIN, (PLANE - 1) * MAIN)], b_ss)
    sent(zs, z_ss)


def shards(tokens, routes, combine_weight, gate_weight, up_weight, down_weight):
    tok, width = tokens.shape
    ff = gate_weight.shape[2]
    fq = ff // NY
    n = CHUNKS
    wide = width + width // CUT
    vm = pltpu.VMEM
    dma = pltpu.SemaphoreType.DMA
    any_space = pl.BlockSpec(memory_space=pl.ANY)
    return pl.pallas_call(
        body,
        out_shape=jax.ShapeDtypeStruct((tok, width), BF16),
        in_specs=[pl.BlockSpec(memory_space=vm)] * 3 + [any_space] * 3,
        out_specs=pl.BlockSpec(memory_space=vm),
        scratch_shapes=[
            vm((NZ, tok, width), BF16),
            vm((NZ, 2 * TOPK, tok), F32),
            vm((NZ, PLANE, tok), F32),
            vm((NZ, PLANE, tok), F32),
            vm((width, 2 * ff), BF16),
            vm((ff, width), BF16),
            vm((NZ, PLANE * MAIN, wide), BF16),
            vm((n, LARGE * UROWS, wide), BF16),
            vm((ROWS, width), BF16),
            vm((2, n, ROWS, fq), BF16),
            vm((2, n, ROWS, fq), BF16),
            vm((2, ROWS, fq), F32),
            vm((2, n, ROWS, 2 * fq), BF16),
            vm((2, n, ROWS, 2 * fq), BF16),
            vm((2, ROWS, 2 * fq), F32),
            vm((n, ROWS, ff), BF16),
            vm((ROWS, width), BF16),
            vm((n, LARGE * UROWS, wide), BF16),
            vm((NZ, PLANE * MAIN, wide), BF16),
            vm((NZ, tok, width), F32),
            vm((NZ - 1, tok, width), BF16),
            vm((NZ - 1, tok, width), BF16),
            dma((3 * NY,)),
            dma,
            dma((NZ - 1,)),
            dma,
            dma((NZ - 1,)),
            dma,
            dma((n, LARGE)),
            dma,
            dma((2, n)),
            dma,
            dma((2, n)),
            dma,
            dma((2, n)),
            dma,
            dma((2, n)),
            dma,
            dma((NZ, NX)),
            dma,
            dma((NZ - 1,)),
        ],
        compiler_params=pltpu.CompilerParams(
            collective_id=0, has_side_effects=True, vmem_limit_bytes=62 * 1024 * 1024
        ),
        cost_estimate=pl.CostEstimate(flops=13 * 10**9, bytes_accessed=10 * 10**6, transcendentals=0),
    )(routes.T, combine_weight.T, tokens, gate_weight[0], up_weight[0], down_weight[0])


def solution(mesh):
    return jax.shard_map(
        shards,
        mesh=mesh,
        in_specs=(
            P("ep", "kv"),
            P("ep", None),
            P("ep", None),
            P("ep", "kv", None),
            P("ep", "kv", None),
            P("ep", None, "kv"),
        ),
        out_specs=P("ep", "kv"),
        check_vma=False,
    )
```

time: 508 us -> 137 us (0.27)
  waiting for transfers between devices: 268 us -> 0 us
  Pallas kernels: 0 us -> 135 us
  blocking collectives: 85.7 us -> 0 us
  local copies, waits for them, and re-layouts: 50.2 us -> 1.67 us
  other arithmetic: 47.9 us -> 0 us
  matrix products: 28 us -> 0 us
  between operations: 13.2 us -> 0.01 us
  starting transfers between devices: 11.3 us -> 0 us
    reduce_scatter x2 -> x0, waiting for transfers between devices: 147 us -> none  [the longest x1 81.7 us: shards(): up_sum = lax.psum_scatter(up_part, 'kv', scatter_dimension=1, tiled=True)]
    pallas_call x0 -> x1, Pallas kernels: none -> 135 us  [shards(): pl.pallas_call(body, out_shape=jax.ShapeDtypeStruct((tok, width), BF16),...]
    all_to_all x1 -> x0, blocking collectives: 85.7 us -> none  [shards(): lax.all_to_all(outgoing, 'ep', split_axis=0, concat_axis=0, tiled=True)]
    all_to_all x1 -> x0, waiting for transfers between devices: 72.4 us -> none  [shards(): lax.all_to_all(expert_rows, 'ep', split_axis=0, concat_axis=0, tiled=True)]
    all_gather x1 -> x0, waiting for transfers between devices: 48.5 us -> none  [shards(): lax.all_gather(hidden, 'kv', axis=1, tiled=True)]
    another operation x3 -> x0, other arithmetic: 36 us -> none
    dot_general x3 -> x0, matrix products: 28 us -> none  [the longest x1 11 us: shards(): up_part = jnp.dot(row_block, w_up, preferred_element_type=jnp.float32)]
    gather x3 -> x0, local copies, waits for them, and re-layouts: 18.4 us -> none  [the longest x2 10.2 us: shards(): tokens[token_slot] * occupied[:, None]]
  transfers between devices with their start and end apart: 4 -> 0, of which waited for: 4 -> 0; matrix products, arithmetic and copies ran while one was open for 2% -> 0% of each run, Pallas kernels for 0% -> 0%
where the time goes in v2:
time: 137 us
  Pallas kernels  135 us (99%)
  local copies, waits for them, and re-layouts  1.67 us (1%)
    pallas_call x1, Pallas kernels, shards(): pl.pallas_call(body, out_shape=jax.ShapeDtypeStruct((tok, width), BF16),...  135 us

profile of v2, /device:TPU:1, one launch (start us, length us, event | category | flops | bytes accessed | tf_op | source)
XLA Modules:
  0.0 136.7 jit_solution(9552031613026369163)
XLA Ops:
  0.0 135.0 %shard_map.64 = bf16[128,1024]{1,0:T(8,128)(2,1)} custom-call(s32[8,128]{1,0:T(8,128)} %bitcast.8, f32[8,128]{1,0:T(8,128)} %bitcast.9, bf16[128,1024]{1,0:T(8,128)(2,1)} %tok_ref.1, bf16[1024,1536]{1,0:T(8,128)(2,1)} %bitcast.5, bf16[1024,1536]{1,0:T(8,128)(2,1)} %bitcast.6, bf16[1536,1024]{1,0:T(8,128)(2,1)} %bitcast.7), custom_call_target="tpu_custom_call" | custom-call | flops 12999999488 | bytes 10000000 | tf_op jit(solution)/shard_map/pallas_call | solution.py:351
  135.0 1.7 %copy.8 = bf16[128,1024]{1,0:T(8,128)(2,1)} copy(bf16[128,1024]{1,0:T(8,128)(2,1)} %shard_map.64) | data formatting | bytes 524288

commit v3 on v2

--- a/solution.py
+++ b/solution.py
@@ -21,16 +21,16 @@
 ORDER = tuple(
     tuple(divmod(unit, 10) for unit in chunk)
     for chunk in (
-        (3, 1),
+        (1, 0),
         (20, 10),
-        (12, 21, 11, 13),
-        (50, 31, 32, 33),
-        (61, 71, 51, 53),
-        (70, 52, 73, 72),
-        (62, 63, 60, 42),
-        (30, 43, 41, 40),
-        (23, 22),
-        (2, 0),
+        (11, 30, 12, 13),
+        (22, 61, 51, 32),
+        (42, 62, 33, 70),
+        (73, 71, 63, 72),
+        (53, 52, 60, 50),
+        (43, 40, 41, 31),
+        (21, 23),
+        (2, 3),
     )
 )
 CHUNKS, SMALL, LARGE = len(ORDER), 2, 4
@@ -40,20 +40,20 @@
 UNIT = NC * (MAIN + TAIL)
 ROWS = LARGE * UNIT
 
-PLANE_IN, COMBINE, LEAVE = 0, 1, 2
+PLANE_IN, COMBINE, LEAVE, SHARE = 0, 1, 2, 3
 FIRST = ()
-AFTER_P = {0: ((PLANE_IN, 1), (PLANE_IN, 2),), 3: ((PLANE_IN, 7),), 8: ((COMBINE, 5), (COMBINE, 7), (LEAVE, 7),), 9: ((LEAVE, 5),)}
-AFTER_A = {9: ((COMBINE, 6), (LEAVE, 6),), 10: ((LEAVE, 4),)}
-AFTER_D = {2: ((PLANE_IN, 5), (PLANE_IN, 6),), 5: ((COMBINE, 1),)}
-AFTER_M = {1: ((PLANE_IN, 3), (PLANE_IN, 4),)}
-AFTER_F = {9: ((COMBINE, 3), (COMBINE, 4), (LEAVE, 3),)}
-LAST = ((LEAVE, 1), (COMBINE, 2), (LEAVE, 2), (COMBINE, 0),)
+AFTER_P = {0: ((PLANE_IN, 1), (PLANE_IN, 2),), 3: ((PLANE_IN, 7),), 5: ((COMBINE, 1),), 8: ((COMBINE, 7), (LEAVE, 7),)}
+AFTER_A = {1: ((PLANE_IN, 3), (PLANE_IN, 4),), 2: ((PLANE_IN, 5), (PLANE_IN, 6),), 9: ((COMBINE, 5), (LEAVE, 5),), 10: ((COMBINE, 3), (LEAVE, 3),)}
+AFTER_D = {}
+AFTER_M = {8: ((COMBINE, 6), (LEAVE, 6),)}
+AFTER_F = {4: ((SHARE, 1), (SHARE, 7),), 5: ((SHARE, 6), (SHARE, 5),), 6: ((SHARE, 4), (SHARE, 3),), 7: ((SHARE, 2), (SHARE, 0),), 9: ((COMBINE, 4), (LEAVE, 4),)}
+LAST = ((COMBINE, 2), (LEAVE, 2), (LEAVE, 1), (COMBINE, 0),)
 
 def body(
     rt_ref, wt_ref, tok_ref, wg_ref, wu_ref, wd_ref, out_ref,
-    tok_all, meta_all, vv, ww, wgu, wdn, sel, xin, xrows, hop_s, hop_r, qf, qs, qr, own, hid, erow, eout, back,
+    rt_own, tok_all, meta_all, vv, ww, shares_all, wgu, wdn, sel, xin, xrows, hop_s, hop_r, qf, qs, qr, own, hid, erow, eout, back,
     zp, zs, zr,
-    w_sem, zt_ss, zt_rs, zm_ss, zm_rs, x_ss, x_rs, hop_ss, hop_rs, q_ss, q_rs, ag_ss, ag_rs,
+    in_sem, w_sem, zt_ss, zt_rs, zm_ss, zm_rs, x_ss, x_rs, hop_ss, hop_rs, q_ss, q_rs, ag_ss, ag_rs,
     fw_ss, fw_rs, b_ss, b_rs, z_ss, z_rs,
 ):
     tok, width = tok_ref.shape
@@ -74,6 +74,8 @@
 
     up_y, down_y = dev(dy=1), dev(dy=-1)
     up_z, down_z = dev(dz=1), dev(dz=-1)
+    plane = [(dx, dc) for dx in range(NX) for dc in range(NC)]
+    mate = {at: dev(dx=at[0], dc=at[1]) for at in plane}
 
     def arrived(dst, rs):
         remote(dst, dst, rs, rs, up_y).wait_recv()
@@ -81,11 +83,18 @@
     def sent(src, ss):
         remote(src, src, ss, ss, up_y).wait_send()
 
-    plane = [(dx, dc) for dx in range(NX) for dc in range(NC)]
     barrier = pltpu.get_barrier_semaphore()
-    partners = [up_y, down_y, up_z, down_z] + [dev(dx=dx, dc=dc) for dx, dc in plane[1:]]
+    partners = [up_y, down_y, up_z, down_z] + [mate[at] for at in plane[1:]]
     for partner in partners:
         pl.semaphore_signal(barrier, inc=1, device_id=partner, device_id_type=MESH)
+
+    inputs = [
+        pltpu.make_async_copy(rt_ref, rt_own, in_sem.at[0]),
+        pltpu.make_async_copy(wt_ref, meta_all.at[0, pl.ds(TOPK, TOPK)], in_sem.at[1]),
+        pltpu.make_async_copy(tok_ref, tok_all.at[0], in_sem.at[2]),
+    ]
+    for load in inputs:
+        load.start()
 
     loads = []
     for r in range(NY):
@@ -120,20 +129,37 @@
             share += jnp.where(same, wt[k : k + 1, :], 0.0)
         earlier = lax.broadcasted_iota(jnp.int32, (tok, tok), 0) < lax.broadcasted_iota(jnp.int32, (tok, tok), 1)
         rank = jnp.dot(hit.astype(BF16), jnp.where(earlier, 1.0, 0.0).astype(BF16), preferred_element_type=F32)
-        vv[p] = jnp.where(hit > 0.5, rank, -1000.0)
+        vv[p] = jnp.where(hit > 0.5, rank, -64.0)
         ww[p] = share
 
     def select(p):
         slot = spread(vv[p])
-
-        def rows(of, cols):
-            return jnp.dot(jnp.where(slot == of, 1.0, 0.0).astype(BF16), tok_all[p, :, cols], preferred_element_type=F32)
-
-        sel[p, :, :width] = rows(main_slot, slice(0, width)).astype(BF16)
-        tail = rows(tail_slot[0], slice(0, block))
-        for b in range(1, CUT):
-            tail += rows(tail_slot[b], slice(b * block, (b + 1) * block))
+        tail = jnp.zeros((PLANE * MAIN, block), F32)
+        first = jnp.where(slot == main_slot, 1.0, 0.0).astype(BF16)
+        for b in range(CUT):
+            cols = slice(b * block, (b + 1) * block)
+            last = jnp.where(slot == tail_slot[b], 1.0, 0.0).astype(BF16)
+            both = jnp.dot(jnp.concatenate([first, last], axis=0), tok_all[p, :, cols], preferred_element_type=F32)
+            sel[p, :, cols] = both[: PLANE * MAIN].astype(BF16)
+            tail += both[PLANE * MAIN :]
         sel[p, :, width:] = tail.astype(BF16)
+
+    def share(p):
+        expand = lax.broadcasted_iota(jnp.int32, (PLANE, PLANE * MAIN), 1) // MAIN
+        expand = jnp.where(expand == lax.broadcasted_iota(jnp.int32, (PLANE, PLANE * MAIN), 0), 1.0, 0.0)
+
+        def by_token(rows):
+            return lax.dot_general(rows, expand, (((0,), (0,)), ((), ())), preferred_element_type=F32)
+
+        weight = ww[p]
+        high = weight.astype(BF16).astype(F32)
+        slot, high, low = by_token(vv[p]), by_token(high), by_token(weight - high)
+        lane = lax.rem(lax.broadcasted_iota(jnp.int32, (tok, PLANE * MAIN), 1), MAIN)
+        wants = [lane] + [jnp.where(lax.rem(lane, CUT) == b, MAIN + lane // CUT, -1) for b in range(CUT)]
+        for n, want in enumerate(wants):
+            same = slot == want.astype(F32)
+            both = jnp.concatenate([jnp.where(same, high, 0.0), jnp.where(same, low, 0.0)], axis=1)
+            shares_all[p, :, 2 * n * PLANE * MAIN : 2 * (n + 1) * PLANE * MAIN] = both.astype(BF16)
 
     def dispatch(p):
         todo = []
@@ -146,7 +172,7 @@
             if dx == 0 and dc == 0:
                 pltpu.make_async_copy(src, dst, x_rs.at[k, a]).start()
             else:
-                remote(src, dst, x_ss, x_rs.at[k, a], dev(dx=dx, dc=dc)).start()
+                remote(src, dst, x_ss, x_rs.at[k, a], mate[dx, dc]).start()
 
     def z_send(p):
         for q in NEXT_HOP[p]:
@@ -238,7 +264,7 @@
             if dx == 0 and dc == 0:
                 pltpu.make_async_copy(src, dst, b_rs.at[p, d]).start()
             else:
-                remote(src, dst, b_ss, b_rs.at[p, d], dev(dx=dx, dc=dc)).start()
+                remote(src, dst, b_ss, b_rs.at[p, d], mate[dx, dc]).start()
 
     def down(i, n):
         arrived(half(i, n, 2, 0), fw_rs.at[0, i])
@@ -258,21 +284,16 @@
     def combine(p):
         for d in range(NX):
             arrived(back.at[p, pl.ds(d * UROWS, UROWS)], b_rs.at[p, d])
-        slot, share = spread(vv[p]), spread(ww[p])
-
-        def weighted(of, cols):
-            exact = jnp.where(slot == of, share, 0.0)
-            high = exact.astype(BF16)
-            low = (exact - high.astype(F32)).astype(BF16)
-            both = lax.dot_general(
-                jnp.concatenate([high, low], axis=1), back[p, :, cols], (((0,), (0,)), ((), ())),
-                preferred_element_type=F32,
+        span = 2 * PLANE * MAIN
+        last = back[p, :, width:]
+        for b in range(CUT):
+            cols = slice(b * block, (b + 1) * block)
+            first = back[p, :, cols]
+            weights = jnp.concatenate(
+                [shares_all[p, :, :span], shares_all[p, :, (b + 1) * span : (b + 2) * span]], axis=1
             )
-            return both[:tok] + both[tok:]
-
-        zp[p] = weighted(main_slot, slice(0, width))
-        for b in range(CUT):
-            zp[p, :, b * block : (b + 1) * block] += weighted(tail_slot[b], slice(width, width + block))
+            rows = jnp.concatenate([first, first, last, last], axis=0)
+            zp[p, :, cols] = jnp.dot(weights, rows, preferred_element_type=F32)
 
     def leave(p):
         out, base, to = (LEFT_OUT, 0, down_z) if p in LEFT_OUT else (RIGHT_OUT, len(LEFT_OUT), up_z)
@@ -284,15 +305,15 @@
         zs[h] = total.astype(BF16)
         remote(zs.at[h], zr.at[h], z_ss, z_rs.at[h], to).start()
 
-    ops = {0: z_arrived, 1: combine, 2: leave}
+    ops = {PLANE_IN: z_arrived, COMBINE: combine, LEAVE: leave, SHARE: share}
 
     def perform(todo):
         for op, p in todo:
             ops[op](p)
 
-    tok_all[0] = tok_ref[...]
-    meta_all[0, 0:TOPK, :] = rt_ref[...].astype(F32)
-    meta_all[0, TOPK : 2 * TOPK, :] = wt_ref[...]
+    for load in inputs:
+        load.wait()
+    meta_all[0, 0:TOPK, :] = rt_own[...].astype(F32)
     prepare(0)
     select(0)
     pl.semaphore_wait(barrier, len(partners))
@@ -351,13 +372,15 @@
     return pl.pallas_call(
         body,
         out_shape=jax.ShapeDtypeStruct((tok, width), BF16),
-        in_specs=[pl.BlockSpec(memory_space=vm)] * 3 + [any_space] * 3,
+        in_specs=[any_space] * 6,
         out_specs=pl.BlockSpec(memory_space=vm),
         scratch_shapes=[
+            vm((TOPK, tok), jnp.int32),
             vm((NZ, tok, width), BF16),
             vm((NZ, 2 * TOPK, tok), F32),
             vm((NZ, PLANE, tok), F32),
             vm((NZ, PLANE, tok), F32),
+            vm((NZ, tok, 2 * (1 + CUT) * PLANE * MAIN), BF16),
             vm((width, 2 * ff), BF16),
             vm((ff, width), BF16),
             vm((NZ, PLANE * MAIN, wide), BF16),
@@ -376,6 +399,7 @@
             vm((NZ, tok, width), F32),
             vm((NZ - 1, tok, width), BF16),
             vm((NZ - 1, tok, width), BF16),
+            dma((3,)),
             dma((3 * NY,)),
             dma,
             dma((NZ - 1,)),

time: 137 us -> 136 us (level)
  no operation moved by 1% of the time
where the time goes in v3:
time: 136 us; the launch traced here: 135 us
  Pallas kernels  134 us (99%)
  local copies, waits for them, and re-layouts  1.67 us (1%)
    pallas_call x1, Pallas kernels, shards(): pl.pallas_call(body, out_shape=jax.ShapeDtypeStruct((tok, width), BF16),...  134 us

profile of v3, /device:TPU:1, one launch (start us, length us, event | category | flops | bytes accessed | tf_op | source)
XLA Modules:
  0.0 135.5 jit_solution(13221541737015033250)
XLA Ops:
  0.0 133.8 %shard_map.64 = bf16[128,1024]{1,0:T(8,128)(2,1)} custom-call(s32[8,128]{1,0:T(8,128)} %bitcast.8, f32[8,128]{1,0:T(8,128)} %bitcast.9, bf16[128,1024]{1,0:T(8,128)(2,1)} %tok_ref.1, bf16[1024,1536]{1,0:T(8,128)(2,1)} %bitcast.5, bf16[1024,1536]{1,0:T(8,128)(2,1)} %bitcast.6, bf16[1536,1024]{1,0:T(8,128)(2,1)} %bitcast.7), custom_call_target="tpu_custom_call" | custom-call | flops 12999999488 | bytes 10000000 | tf_op jit(solution)/shard_map/pallas_call | solution.py:372
  133.8 1.7 %copy.8 = bf16[128,1024]{1,0:T(8,128)(2,1)} copy(bf16[128,1024]{1,0:T(8,128)(2,1)} %shard_map.64) | data formatting | bytes 524288

commit v4 on v3

--- a/solution.py
+++ b/solution.py
@@ -21,20 +21,19 @@
 ORDER = tuple(
     tuple(divmod(unit, 10) for unit in chunk)
     for chunk in (
-        (1, 0),
-        (20, 10),
-        (11, 30, 12, 13),
-        (22, 61, 51, 32),
-        (42, 62, 33, 70),
-        (73, 71, 63, 72),
-        (53, 52, 60, 50),
-        (43, 40, 41, 31),
-        (21, 23),
-        (2, 3),
+        (0, 3),
+        (1, 10),
+        (13, 11, 21, 12),
+        (41, 60, 50, 51),
+        (70, 63, 71, 61),
+        (62, 53, 72, 73),
+        (52, 31, 42, 43),
+        (32, 40, 30, 33),
+        (23, 22),
+        (2, 20),
     )
 )
 CHUNKS, SMALL, LARGE = len(ORDER), 2, 4
-LOW, HIGH = 2, CHUNKS - 2
 POS = {unit: (k, a) for k, units in enumerate(ORDER) for a, unit in enumerate(units)}
 UROWS = NC * MAIN
 UNIT = NC * (MAIN + TAIL)
@@ -42,12 +41,22 @@
 
 PLANE_IN, COMBINE, LEAVE, SHARE = 0, 1, 2, 3
 FIRST = ()
-AFTER_P = {0: ((PLANE_IN, 1), (PLANE_IN, 2),), 3: ((PLANE_IN, 7),), 5: ((COMBINE, 1),), 8: ((COMBINE, 7), (LEAVE, 7),)}
-AFTER_A = {1: ((PLANE_IN, 3), (PLANE_IN, 4),), 2: ((PLANE_IN, 5), (PLANE_IN, 6),), 9: ((COMBINE, 5), (LEAVE, 5),), 10: ((COMBINE, 3), (LEAVE, 3),)}
-AFTER_D = {}
-AFTER_M = {8: ((COMBINE, 6), (LEAVE, 6),)}
-AFTER_F = {4: ((SHARE, 1), (SHARE, 7),), 5: ((SHARE, 6), (SHARE, 5),), 6: ((SHARE, 4), (SHARE, 3),), 7: ((SHARE, 2), (SHARE, 0),), 9: ((COMBINE, 4), (LEAVE, 4),)}
-LAST = ((COMBINE, 2), (LEAVE, 2), (LEAVE, 1), (COMBINE, 0),)
+ALL_STEPS = tuple(range(CHUNKS + 2))
+EARLY_A = (1, 2, 3, 4, 5, 6, 7, 8, 9, 10)
+EARLY_M = (0, 1, 2, 3, 5, 8, 9)
+EARLY_F = (1,)
+LATE_A = ()
+LATE_M = (4, 6, 7)
+LATE_F = (2, 3, 4, 5, 6, 7, 8, 9, 10)
+AFTER_P = {0: ((PLANE_IN, 1),), 6: ((SHARE, 3),), 7: ((SHARE, 7),), 8: ((COMBINE, 6),)}
+AFTER_EARLY_A = {2: ((PLANE_IN, 5),), 3: ((SHARE, 2), (PLANE_IN, 7)), 8: ((COMBINE, 7), (LEAVE, 6), (LEAVE, 7)), 9: ((COMBINE, 5), (LEAVE, 5)), 10: ((LEAVE, 4),)}
+AFTER_EARLY_M = {0: ((PLANE_IN, 2),), 1: ((PLANE_IN, 3), (PLANE_IN, 4)), 2: ((PLANE_IN, 6),), 5: ((SHARE, 1),)}
+AFTER_EARLY_F = {}
+AFTER_D = {10: ((COMBINE, 3), (LEAVE, 3))}
+AFTER_A = {}
+AFTER_M = {4: ((SHARE, 5),), 7: ((SHARE, 4), (SHARE, 6), (SHARE, 0))}
+AFTER_F = {6: ((COMBINE, 1),), 9: ((COMBINE, 4),)}
+LAST = ((COMBINE, 2), (LEAVE, 2), (LEAVE, 1), (COMBINE, 0))
 
 def body(
     rt_ref, wt_ref, tok_ref, wg_ref, wu_ref, wd_ref, out_ref,
@@ -307,6 +316,12 @@
 
     ops = {PLANE_IN: z_arrived, COMBINE: combine, LEAVE: leave, SHARE: share}
 
+    def one_of(s, steps):
+        hit = s == steps[0]
+        for t in steps[1:]:
+            hit = jnp.logical_or(hit, s == t)
+        return hit
+
     def perform(todo):
         for op, p in todo:
             ops[op](p)
@@ -324,20 +339,21 @@
         load.wait()
 
     def step(s, carry):
-        for run, lag, table in (
-            (partials, 0, AFTER_P),
-            (activate, 1, AFTER_A),
-            (down, 2, AFTER_D),
-            (middle, 0, AFTER_M),
-            (forward, 1, AFTER_F),
+        for run, lag, steps, table in (
+            (partials, 0, ALL_STEPS, AFTER_P),
+            (activate, 1, EARLY_A, AFTER_EARLY_A),
+            (middle, 0, EARLY_M, AFTER_EARLY_M),
+            (forward, 1, EARLY_F, AFTER_EARLY_F),
+            (down, 2, ALL_STEPS, AFTER_D),
+            (activate, 1, LATE_A, AFTER_A),
+            (middle, 0, LATE_M, AFTER_M),
+            (forward, 1, LATE_F, AFTER_F),
         ):
             i = s - lag
-            large = jnp.logical_and(i >= LOW, i < HIGH)
-            small = jnp.logical_or(
-                jnp.logical_and(i >= 0, i < LOW), jnp.logical_and(i >= HIGH, i < CHUNKS)
-            )
-            pl.when(large)(lambda run=run, i=i: run(i, LARGE))
-            pl.when(small)(lambda run=run, i=i: run(i, SMALL))
+            for n in (LARGE, SMALL):
+                at = [t for t in steps if 0 <= t - lag < CHUNKS and len(ORDER[t - lag]) == n]
+                if at:
+                    pl.when(one_of(s, at))(lambda run=run, i=i, n=n: run(i, n))
             for at, todo in table.items():
                 pl.when(s == at)(lambda todo=todo: perform(todo))
         return carry
@@ -371,7 +387,7 @@
     any_space = pl.BlockSpec(memory_space=pl.ANY)
     return pl.pallas_call(
         body,
-        out_shape=jax.ShapeDtypeStruct((tok, width), BF16),
+        out_shape=vm((tok, width), BF16),
         in_specs=[any_space] * 6,
         out_specs=pl.BlockSpec(memory_space=vm),
         scratch_shapes=[
@@ -421,7 +437,7 @@
             dma((NZ - 1,)),
         ],
         compiler_params=pltpu.CompilerParams(
-            collective_id=0, has_side_effects=True, vmem_limit_bytes=62 * 1024 * 1024
+            collective_id=0, has_side_effects=True, vmem_limit_bytes=60 * 1024 * 1024
         ),
         cost_estimate=pl.CostEstimate(flops=13 * 10**9, bytes_accessed=10 * 10**6, transcendentals=0),
     )(routes.T, combine_weight.T, tokens, gate_weight[0], up_weight[0], down_weight[0])

time: 136 us -> 138 us (1.015)
  Pallas kernels: 134 us -> 137 us
    pallas_call x1, Pallas kernels: 134 us -> 137 us  [shards(): pl.pallas_call(body, out_shape=vm((tok, width), BF16), in_specs=[any_spac...]
where the time goes in v4:
time: 138 us; the launch traced here: 137 us
  Pallas kernels  137 us (99%)
    pallas_call x1, Pallas kernels, shards(): pl.pallas_call(body, out_shape=vm((tok, width), BF16), in_specs=[any_spac...  137 us

profile of v4, /device:TPU:1, one launch (start us, length us, event | category | flops | bytes accessed | tf_op | source)
XLA Modules:
  0.0 137.5 jit_solution(10825527408718289579)
XLA Ops:
  0.0 136.8 %shard_map.64 = bf16[128,1024]{1,0:T(8,128)(2,1)S(1)} custom-call(s32[8,128]{1,0:T(8,128)} %bitcast.8, f32[8,128]{1,0:T(8,128)} %bitcast.9, bf16[128,1024]{1,0:T(8,128)(2,1)} %tok_ref.1, bf16[1024,1536]{1,0:T(8,128)(2,1)} %bitcast.5, bf16[1024,1536]{1,0:T(8,128)(2,1)} %bitcast.6, bf16[1536,1024]{1,0:T(8,128)(2,1)} %bitcast.7), custom_call_target="tpu_custom_call" | custom-call | flops 12999999488 | bytes 10000000 | tf_op jit(solution)/shard_map/pallas_call | solution.py:388
  136.8 0.7 copy.8

commit v5 on v4

--- a/solution.py
+++ b/solution.py
@@ -17,6 +17,7 @@
 RIGHT_OUT = (6, 4, 2)
 
 MAIN, TAIL, CUT = 16, 4, 4
+TILE = 256
 
 ORDER = tuple(
     tuple(divmod(unit, 10) for unit in chunk)
@@ -60,7 +61,7 @@
 
 def body(
     rt_ref, wt_ref, tok_ref, wg_ref, wu_ref, wd_ref, out_ref,
-    rt_own, tok_all, meta_all, vv, ww, shares_all, wgu, wdn, sel, xin, xrows, hop_s, hop_r, qf, qs, qr, own, hid, erow, eout, back,
+    rt_own, tok_all, meta_all, vv, ww, shares_all, wgu, wdn, sel, xin, xrows, hop_s, hop_r, qf, qs, qr, own, hid, eout, back,
     zp, zs, zr,
     in_sem, w_sem, zt_ss, zt_rs, zm_ss, zm_rs, x_ss, x_rs, hop_ss, hop_rs, q_ss, q_rs, ag_ss, ag_rs,
     fw_ss, fw_rs, b_ss, b_rs, z_ss, z_rs,
@@ -216,27 +217,47 @@
             tail = jnp.dot(picks(n, b, 0), xin[i, :whole, width:], preferred_element_type=F32)
             xrows[whole:rows, b * block : (b + 1) * block] = tail.astype(BF16)
 
-        def part(r):
-            return jnp.dot(xrows[:rows], wgu[:, 2 * r * fq : 2 * (r + 1) * fq], preferred_element_type=F32)
-
-        far = part(2)
-        hop_s[0, i, :rows] = far[:, :fq].astype(BF16)
-        hop_s[1, i, :rows] = far[:, fq:].astype(BF16)
+        def part(r, sink):
+            for at in range(0, 2 * fq, TILE):
+                cols = slice(2 * r * fq + at, 2 * r * fq + at + TILE)
+                tile = jnp.dot(xrows[:rows], wgu[:, cols], preferred_element_type=F32)
+                for which in range(2):
+                    low, high = max(at, which * fq), min(at + TILE, (which + 1) * fq)
+                    if low < high:
+                        sink(which, slice(low - which * fq, high - which * fq), tile[:, low - at : high - at])
+
+        def far(which, cols, tile):
+            hop_s[which, i, :rows, cols] = tile.astype(BF16)
+
+        def next_to(d):
+            def sink(which, cols, tile):
+                if which == d:
+                    qf[d, :rows, cols] = tile
+                else:
+                    qs[d, i, :rows, which * fq + cols.start : which * fq + cols.stop] = tile.astype(BF16)
+
+            return sink
+
+        def keep(which, cols, tile):
+            own[lax.rem(i, 2), :rows, which * fq + cols.start : which * fq + cols.stop] = tile
+
+        part(2, far)
         send_y(hop_s, hop_r, i, n, hop_ss, hop_rs)
-        above = part(1)
-        qf[0, :rows] = above[:, :fq]
-        qs[0, i, :rows, fq:] = above[:, fq:].astype(BF16)
-        below = part(3)
-        qs[1, i, :rows, :fq] = below[:, :fq].astype(BF16)
-        qf[1, :rows] = below[:, fq:]
-        own[lax.rem(i, 2), :rows] = part(0)
+        part(1, next_to(0))
+        part(3, next_to(1))
+        part(0, keep)
+
+    def blocks(rows):
+        step = rows // 5
+        return [slice(at, at + step) for at in range(0, rows, step)]
 
     def middle(i, n):
         rows = n * UNIT
         for d, to in enumerate((up_y, down_y)):
             arrived(hop_r.at[d, i, pl.ds(0, rows)], hop_rs.at[d, i])
-            total = qf[d, :rows] + hop_r[d, i, :rows].astype(F32)
-            qs[d, i, :rows, d * fq : (d + 1) * fq] = total.astype(BF16)
+            for rs in blocks(rows):
+                total = qf[d, rs] + hop_r[d, i, rs].astype(F32)
+                qs[d, i, rs, d * fq : (d + 1) * fq] = total.astype(BF16)
             part = pl.ds(0, rows)
             remote(qs.at[d, i, part], qr.at[d, i, part], q_ss, q_rs.at[d, i], to).start()
 
@@ -252,9 +273,14 @@
         rows = n * UNIT
         for d in range(2):
             arrived(qr.at[d, i, pl.ds(0, rows)], q_rs.at[d, i])
-        total = own[lax.rem(i, 2), :rows] + qr[0, i, :rows].astype(F32) + qr[1, i, :rows].astype(F32)
-        gate, up = total[:, :fq], total[:, fq:]
-        hid[i, :rows, :fq] = (gate / (1.0 + jnp.exp(-gate)) * up).astype(BF16)
+        for rs in blocks(rows):
+
+            def total(which):
+                cols = slice(which * fq, (which + 1) * fq)
+                return own[lax.rem(i, 2), rs, cols] + qr[0, i, rs, cols].astype(F32) + qr[1, i, rs, cols].astype(F32)
+
+            gate = total(0)
+            hid[i, rs, :fq] = (gate / (1.0 + jnp.exp(-gate)) * total(1)).astype(BF16)
         remote(quarter(i, n, 0), quarter(i, n, 3), ag_ss, ag_rs.at[0, i], up_y).start()
         remote(quarter(i, n, 0), quarter(i, n, 1), ag_ss, ag_rs.at[1, i], down_y).start()
 
@@ -279,12 +305,12 @@
         arrived(half(i, n, 2, 0), fw_rs.at[0, i])
         arrived(half(i, n, 2, 1), fw_rs.at[1, i])
         rows, whole = n * UNIT, n * UROWS
-        erow[:rows] = jnp.dot(hid[i, :rows], wdn[...], preferred_element_type=F32).astype(BF16)
-        eout[i, :whole, :width] = erow[:whole]
         tail = jnp.zeros((whole, block), F32)
         for b in range(CUT):
-            last = erow[whole:rows, b * block : (b + 1) * block]
-            tail += jnp.dot(picks(n, b, 1), last, preferred_element_type=F32)
+            cols = slice(b * block, (b + 1) * block)
+            part = jnp.dot(hid[i, :rows], wdn[:, cols], preferred_element_type=F32).astype(BF16)
+            eout[i, :whole, cols] = part[:whole]
+            tail += jnp.dot(picks(n, b, 1), part[whole:], preferred_element_type=F32)
         eout[i, :whole, width:] = tail.astype(BF16)
         for k in range(CHUNKS):
             if len(ORDER[k]) == n:
@@ -304,14 +330,19 @@
             rows = jnp.concatenate([first, first, last, last], axis=0)
             zp[p, :, cols] = jnp.dot(weights, rows, preferred_element_type=F32)
 
+    def blocks4(rows):
+        return [slice(at, at + rows // 4) for at in range(0, rows, rows // 4)]
+
     def leave(p):
         out, base, to = (LEFT_OUT, 0, down_z) if p in LEFT_OUT else (RIGHT_OUT, len(LEFT_OUT), up_z)
         h = base + out.index(p)
-        total = zp[p]
         if h > base:
             arrived(zr.at[h - 1], z_rs.at[h - 1])
-            total = total + zr[h - 1].astype(F32)
-        zs[h] = total.astype(BF16)
+        for rs in blocks4(tok):
+            total = zp[p, rs]
+            if h > base:
+                total = total + zr[h - 1, rs].astype(F32)
+            zs[h, rs] = total.astype(BF16)
         remote(zs.at[h], zr.at[h], z_ss, z_rs.at[h], to).start()
 
     ops = {PLANE_IN: z_arrived, COMBINE: combine, LEAVE: leave, SHARE: share}
@@ -363,7 +394,8 @@
     last_left, last_right = len(LEFT_OUT) - 1, len(LEFT_OUT) + len(RIGHT_OUT) - 1
     arrived(zr.at[last_right], z_rs.at[last_right])
     arrived(zr.at[last_left], z_rs.at[last_left])
-    out_ref[...] = (zp[0] + zr[last_left].astype(F32) + zr[last_right].astype(F32)).astype(BF16)
+    for rs in blocks4(tok):
+        out_ref[rs] = (zp[0, rs] + zr[last_left, rs].astype(F32) + zr[last_right, rs].astype(F32)).astype(BF16)
 
     sent(meta_all.at[pl.ds(1, NZ - 1)], zm_ss)
     sent(tok_all.at[pl.ds(1, NZ - 1)], zt_ss)
@@ -409,7 +441,6 @@
             vm((2, n, ROWS, 2 * fq), BF16),
             vm((2, ROWS, 2 * fq), F32),
             vm((n, ROWS, ff), BF16),
-            vm((ROWS, width), BF16),
             vm((n, LARGE * UROWS, wide), BF16),
             vm((NZ, PLANE * MAIN, wide), BF16),
             vm((NZ, tok, width), F32),

time: 138 us -> 138 us (level)
  no operation moved by 1% of the time
where the time goes in v5:
time: 138 us
  Pallas kernels  137 us (99%)
    pallas_call x1, Pallas kernels, shards(): pl.pallas_call(body, out_shape=vm((tok, width), BF16), in_specs=[any_spac...  137 us

profile of v5, /device:TPU:1, one launch (start us, length us, event | category | flops | bytes accessed | tf_op | source)
XLA Modules:
  0.0 137.9 jit_solution(6298986714476218128)
XLA Ops:
  0.0 137.2 %shard_map.64 = bf16[128,1024]{1,0:T(8,128)(2,1)S(1)} custom-call(s32[8,128]{1,0:T(8,128)} %bitcast.8, f32[8,128]{1,0:T(8,128)} %bitcast.9, bf16[128,1024]{1,0:T(8,128)(2,1)} %tok_ref.1, bf16[1024,1536]{1,0:T(8,128)(2,1)} %bitcast.5, bf16[1024,1536]{1,0:T(8,128)(2,1)} %bitcast.6, bf16[1536,1024]{1,0:T(8,128)(2,1)} %bitcast.7), custom_call_target="tpu_custom_call" | custom-call | flops 12999999488 | bytes 10000000 | tf_op jit(solution)/shard_map/pallas_call | solution.py:420
  137.2 0.7 copy.8

commit v6 on v4

--- a/solution.py
+++ b/solution.py
@@ -21,16 +21,16 @@
 ORDER = tuple(
     tuple(divmod(unit, 10) for unit in chunk)
     for chunk in (
-        (0, 3),
-        (1, 10),
-        (13, 11, 21, 12),
-        (41, 60, 50, 51),
-        (70, 63, 71, 61),
-        (62, 53, 72, 73),
-        (52, 31, 42, 43),
-        (32, 40, 30, 33),
-        (23, 22),
-        (2, 20),
+        (3, 0),
+        (20, 10),
+        (11, 23, 12, 13),
+        (41, 31, 50, 43),
+        (73, 60, 61, 62),
+        (71, 72, 63, 32),
+        (70, 51, 52, 53),
+        (33, 40, 30, 42),
+        (22, 21),
+        (2, 1),
     )
 )
 CHUNKS, SMALL, LARGE = len(ORDER), 2, 4
@@ -39,31 +39,34 @@
 UNIT = NC * (MAIN + TAIL)
 ROWS = LARGE * UNIT
 
-PLANE_IN, COMBINE, LEAVE, SHARE = 0, 1, 2, 3
+FAR = (2, 1)
+RELAYED = tuple(sorted(p for chunk in ORDER[:-2] for p, dx in chunk if dx == 2))
+
+PLANE_IN, COMBINE, LEAVE, SHARE, RELAY_OUT, RELAY_BACK = range(6)
 FIRST = ()
 ALL_STEPS = tuple(range(CHUNKS + 2))
 EARLY_A = (1, 2, 3, 4, 5, 6, 7, 8, 9, 10)
-EARLY_M = (0, 1, 2, 3, 5, 8, 9)
+EARLY_M = (0, 1, 2, 3, 5, 7)
 EARLY_F = (1,)
 LATE_A = ()
-LATE_M = (4, 6, 7)
+LATE_M = (4, 6, 8, 9)
 LATE_F = (2, 3, 4, 5, 6, 7, 8, 9, 10)
-AFTER_P = {0: ((PLANE_IN, 1),), 6: ((SHARE, 3),), 7: ((SHARE, 7),), 8: ((COMBINE, 6),)}
-AFTER_EARLY_A = {2: ((PLANE_IN, 5),), 3: ((SHARE, 2), (PLANE_IN, 7)), 8: ((COMBINE, 7), (LEAVE, 6), (LEAVE, 7)), 9: ((COMBINE, 5), (LEAVE, 5)), 10: ((LEAVE, 4),)}
-AFTER_EARLY_M = {0: ((PLANE_IN, 2),), 1: ((PLANE_IN, 3), (PLANE_IN, 4)), 2: ((PLANE_IN, 6),), 5: ((SHARE, 1),)}
+AFTER_P = {0: ((PLANE_IN, 1),), 2: ((RELAY_OUT, 0),), 3: ((SHARE, 3),), 5: ((RELAY_OUT, 2), (RELAY_OUT, 5)), 8: ((RELAY_BACK, 6),)}
+AFTER_EARLY_A = {1: ((RELAY_OUT, 1),), 3: ((RELAY_OUT, 6),), 4: ((RELAY_OUT, 7),), 5: ((RELAY_BACK, 1),), 7: ((SHARE, 4),), 8: ((SHARE, 1), (RELAY_BACK, 7)), 9: ((RELAY_BACK, 3), (COMBINE, 5))}
+AFTER_EARLY_M = {0: ((PLANE_IN, 2),), 1: ((PLANE_IN, 3), (PLANE_IN, 4)), 2: ((PLANE_IN, 5), (PLANE_IN, 6)), 3: ((PLANE_IN, 7), (SHARE, 7))}
 AFTER_EARLY_F = {}
-AFTER_D = {10: ((COMBINE, 3), (LEAVE, 3))}
+AFTER_D = {10: ((COMBINE, 3), (COMBINE, 4), (LEAVE, 4), (LEAVE, 3))}
 AFTER_A = {}
-AFTER_M = {4: ((SHARE, 5),), 7: ((SHARE, 4), (SHARE, 6), (SHARE, 0))}
-AFTER_F = {6: ((COMBINE, 1),), 9: ((COMBINE, 4),)}
+AFTER_M = {8: ((COMBINE, 7), (LEAVE, 7), (COMBINE, 6), (SHARE, 0)), 9: ((LEAVE, 5), (RELAY_BACK, 4))}
+AFTER_F = {3: ((RELAY_OUT, 3),), 4: ((RELAY_OUT, 4),), 6: ((SHARE, 2), (SHARE, 5), (SHARE, 6)), 8: ((RELAY_BACK, 5), (LEAVE, 6)), 10: ((COMBINE, 1),)}
 LAST = ((COMBINE, 2), (LEAVE, 2), (LEAVE, 1), (COMBINE, 0))
 
 def body(
     rt_ref, wt_ref, tok_ref, wg_ref, wu_ref, wd_ref, out_ref,
     rt_own, tok_all, meta_all, vv, ww, shares_all, wgu, wdn, sel, xin, xrows, hop_s, hop_r, qf, qs, qr, own, hid, erow, eout, back,
-    zp, zs, zr,
+    zp, zs, zr, out_by, back_by,
     in_sem, w_sem, zt_ss, zt_rs, zm_ss, zm_rs, x_ss, x_rs, hop_ss, hop_rs, q_ss, q_rs, ag_ss, ag_rs,
-    fw_ss, fw_rs, b_ss, b_rs, z_ss, z_rs,
+    fw_ss, fw_rs, b_ss, b_rs, z_ss, z_rs, out_ss, out_rs, home_ss, home_rs,
 ):
     tok, width = tok_ref.shape
     ff = wg_ref.shape[1]
@@ -180,8 +183,21 @@
             dst = xin.at[k, pl.ds(a * UROWS + dc * MAIN, MAIN)]
             if dx == 0 and dc == 0:
                 pltpu.make_async_copy(src, dst, x_rs.at[k, a]).start()
+            elif (dx, dc) == FAR:
+                remote(src, out_by.at[p], x_ss, out_rs.at[p], mate[3, 0]).start()
             else:
                 remote(src, dst, x_ss, x_rs.at[k, a], mate[dx, dc]).start()
+
+    def relay_out(p):
+        k, a = POS[p, 2]
+        arrived(out_by.at[p], out_rs.at[p])
+        dst = xin.at[k, pl.ds(a * UROWS + MAIN, MAIN)]
+        remote(out_by.at[p], dst, out_ss, x_rs.at[k, a], mate[3, 1]).start()
+
+    def relay_back(p):
+        arrived(back_by.at[p], home_rs.at[p])
+        dst = back.at[p, pl.ds((2 * NC + 1) * MAIN, MAIN)]
+        remote(back_by.at[p], dst, home_ss, b_rs.at[p, 2], mate[3, 1]).start()
 
     def z_send(p):
         for q in NEXT_HOP[p]:
@@ -272,6 +288,8 @@
             dst = back.at[p, pl.ds((d * NC + dc) * MAIN, MAIN)]
             if dx == 0 and dc == 0:
                 pltpu.make_async_copy(src, dst, b_rs.at[p, d]).start()
+            elif (dx, dc) == FAR and p in RELAYED:
+                remote(src, back_by.at[p], b_ss, home_rs.at[p], mate[3, 0]).start()
             else:
                 remote(src, dst, b_ss, b_rs.at[p, d], mate[dx, dc]).start()
 
@@ -314,7 +332,7 @@
         zs[h] = total.astype(BF16)
         remote(zs.at[h], zr.at[h], z_ss, z_rs.at[h], to).start()
 
-    ops = {PLANE_IN: z_arrived, COMBINE: combine, LEAVE: leave, SHARE: share}
+    ops = {PLANE_IN: z_arrived, COMBINE: combine, LEAVE: leave, SHARE: share, RELAY_OUT: relay_out, RELAY_BACK: relay_back}
 
     def one_of(s, steps):
         hit = s == steps[0]
@@ -374,6 +392,8 @@
     sent(hop_s.at[0, pl.ds(0, NZ)], fw_ss)
     sent(sel.at[:, pl.ds(MAIN, (PLANE - 1) * MAIN)], b_ss)
     sent(zs, z_ss)
+    sent(out_by, out_ss)
+    sent(back_by.at[pl.ds(0, len(RELAYED))], home_ss)
 
 
 def shards(tokens, routes, combine_weight, gate_weight, up_weight, down_weight):
@@ -415,6 +435,8 @@
             vm((NZ, tok, width), F32),
             vm((NZ - 1, tok, width), BF16),
             vm((NZ - 1, tok, width), BF16),
+            vm((NZ, MAIN, wide), BF16),
+            vm((NZ, MAIN, wide), BF16),
             dma((3,)),
             dma((3 * NY,)),
             dma,
@@ -435,6 +457,10 @@
             dma((NZ, NX)),
             dma,
             dma((NZ - 1,)),
+            dma,
+            dma((NZ,)),
+            dma,
+            dma((NZ,)),
         ],
         compiler_params=pltpu.CompilerParams(
             collective_id=0, has_side_effects=True, vmem_limit_bytes=60 * 1024 * 1024

time: 138 us -> 138 us (level)
  no operation moved by 1% of the time
where the time goes in v6:
time: 138 us
  Pallas kernels  137 us (99%)
    pallas_call x1, Pallas kernels, shards(): pl.pallas_call(body, out_shape=vm((tok, width), BF16), in_specs=[any_spac...  137 us

profile of v6, /device:TPU:1, one launch (start us, length us, event | category | flops | bytes accessed | tf_op | source)
XLA Modules:
  0.0 137.9 jit_solution(2707447685185255237)
XLA Ops:
  0.0 137.2 %shard_map.64 = bf16[128,1024]{1,0:T(8,128)(2,1)S(1)} custom-call(s32[8,128]{1,0:T(8,128)} %bitcast.8, f32[8,128]{1,0:T(8,128)} %bitcast.9, bf16[128,1024]{1,0:T(8,128)(2,1)} %tok_ref.1, bf16[1024,1536]{1,0:T(8,128)(2,1)} %bitcast.5, bf16[1024,1536]{1,0:T(8,128)(2,1)} %bitcast.6, bf16[1536,1024]{1,0:T(8,128)(2,1)} %bitcast.7), custom_call_target="tpu_custom_call" | custom-call | flops 12999999488 | bytes 10000000 | tf_op jit(solution)/shard_map/pallas_call | solution.py:408
  137.2 0.7 copy.8

commit v7 on v4

--- a/solution.py
+++ b/solution.py
@@ -202,10 +202,9 @@
         few, many = lax.broadcasted_iota(jnp.int32, shape, axis), lax.broadcasted_iota(jnp.int32, shape, 1 - axis)
         return jnp.where(many == few * CUT + b, 1.0, 0.0).astype(BF16)
 
-    def send_y(ref, recv, i, n, ss, rs):
-        for d, to in enumerate((up_y, down_y)):
-            part = pl.ds(0, n * UNIT)
-            remote(ref.at[d, i, part], recv.at[d, i, part], ss, rs.at[d, i], to).start()
+    def parts(n):
+        first = -(-n * UNIT // 32) * 16
+        return [(0, first), (first, n * UNIT)]
 
     def partials(i, n):
         for a in range(n):
@@ -222,7 +221,10 @@
         far = part(2)
         hop_s[0, i, :rows] = far[:, :fq].astype(BF16)
         hop_s[1, i, :rows] = far[:, fq:].astype(BF16)
-        send_y(hop_s, hop_r, i, n, hop_ss, hop_rs)
+        for h, (low, high) in enumerate(parts(n)):
+            at = pl.ds(low, high - low)
+            for d, to in enumerate((up_y, down_y)):
+                remote(hop_s.at[d, i, at], hop_r.at[d, i, at], hop_ss, hop_rs.at[d, i, h], to).start()
         above = part(1)
         qf[0, :rows] = above[:, :fq]
         qs[0, i, :rows, fq:] = above[:, fq:].astype(BF16)
@@ -232,36 +234,33 @@
         own[lax.rem(i, 2), :rows] = part(0)
 
     def middle(i, n):
-        rows = n * UNIT
-        for d, to in enumerate((up_y, down_y)):
-            arrived(hop_r.at[d, i, pl.ds(0, rows)], hop_rs.at[d, i])
-            total = qf[d, :rows] + hop_r[d, i, :rows].astype(F32)
-            qs[d, i, :rows, d * fq : (d + 1) * fq] = total.astype(BF16)
-            part = pl.ds(0, rows)
-            remote(qs.at[d, i, part], qr.at[d, i, part], q_ss, q_rs.at[d, i], to).start()
-
-    def quarter(i, n, r):
-        return hid.at[i, pl.ds(0, n * UNIT), pl.ds(r * fq, fq)]
+        for h, (low, high) in enumerate(parts(n)):
+            at, rs = pl.ds(low, high - low), slice(low, high)
+            for d, to in enumerate((up_y, down_y)):
+                arrived(hop_r.at[d, i, at], hop_rs.at[d, i, h])
+                total = qf[d, rs] + hop_r[d, i, rs].astype(F32)
+                qs[d, i, rs, d * fq : (d + 1) * fq] = total.astype(BF16)
+                remote(qs.at[d, i, at], qr.at[d, i, at], q_ss, q_rs.at[d, i, h], to).start()
 
     def half(i, n, r, h):
-        first = -(-n * UNIT // 32) * 16
-        at = pl.ds(0, first) if h == 0 else pl.ds(first, n * UNIT - first)
-        return hid.at[i, at, pl.ds(r * fq, fq)]
+        low, high = parts(n)[h]
+        return hid.at[i, pl.ds(low, high - low), pl.ds(r * fq, fq)]
 
     def activate(i, n):
-        rows = n * UNIT
-        for d in range(2):
-            arrived(qr.at[d, i, pl.ds(0, rows)], q_rs.at[d, i])
-        total = own[lax.rem(i, 2), :rows] + qr[0, i, :rows].astype(F32) + qr[1, i, :rows].astype(F32)
-        gate, up = total[:, :fq], total[:, fq:]
-        hid[i, :rows, :fq] = (gate / (1.0 + jnp.exp(-gate)) * up).astype(BF16)
-        remote(quarter(i, n, 0), quarter(i, n, 3), ag_ss, ag_rs.at[0, i], up_y).start()
-        remote(quarter(i, n, 0), quarter(i, n, 1), ag_ss, ag_rs.at[1, i], down_y).start()
+        for h, (low, high) in enumerate(parts(n)):
+            at, rs = pl.ds(low, high - low), slice(low, high)
+            for d in range(2):
+                arrived(qr.at[d, i, at], q_rs.at[d, i, h])
+            total = own[lax.rem(i, 2), rs] + qr[0, i, rs].astype(F32) + qr[1, i, rs].astype(F32)
+            gate, up = total[:, :fq], total[:, fq:]
+            hid[i, rs, :fq] = (gate / (1.0 + jnp.exp(-gate)) * up).astype(BF16)
+            remote(half(i, n, 0, h), half(i, n, 3, h), ag_ss, ag_rs.at[0, i, h], up_y).start()
+            remote(half(i, n, 0, h), half(i, n, 1, h), ag_ss, ag_rs.at[1, i, h], down_y).start()
 
     def forward(i, n):
-        arrived(quarter(i, n, 3), ag_rs.at[0, i])
+        arrived(half(i, n, 3, 0), ag_rs.at[0, i, 0])
         remote(half(i, n, 3, 0), half(i, n, 2, 0), fw_ss, fw_rs.at[0, i], up_y).start()
-        arrived(quarter(i, n, 1), ag_rs.at[1, i])
+        arrived(half(i, n, 1, 1), ag_rs.at[1, i, 1])
         remote(half(i, n, 1, 1), half(i, n, 2, 1), fw_ss, fw_rs.at[1, i], down_y).start()
 
     def send_back(k):
@@ -276,6 +275,8 @@
                 remote(src, dst, b_ss, b_rs.at[p, d], mate[dx, dc]).start()
 
     def down(i, n):
+        arrived(half(i, n, 3, 1), ag_rs.at[0, i, 1])
+        arrived(half(i, n, 1, 0), ag_rs.at[1, i, 0])
         arrived(half(i, n, 2, 0), fw_rs.at[0, i])
         arrived(half(i, n, 2, 1), fw_rs.at[1, i])
         rows, whole = n * UNIT, n * UROWS
@@ -424,11 +425,11 @@
             dma,
             dma((n, LARGE)),
             dma,
-            dma((2, n)),
-            dma,
-            dma((2, n)),
-            dma,
-            dma((2, n)),
+            dma((2, n, 2)),
+            dma,
+            dma((2, n, 2)),
+            dma,
+            dma((2, n, 2)),
             dma,
             dma((2, n)),
             dma,

time: 138 us -> 135 us (0.978)
  Pallas kernels: 137 us -> 135 us
    pallas_call x1, Pallas kernels: 137 us -> 135 us  [shards(): pl.pallas_call(body, out_shape=vm((tok, width), BF16), in_specs=[any_spac...]
where the time goes in v7:
time: 135 us
  Pallas kernels  135 us (100%)
    pallas_call x1, Pallas kernels, shards(): pl.pallas_call(body, out_shape=vm((tok, width), BF16), in_specs=[any_spac...  135 us

profile of v7, /device:TPU:1, one launch (start us, length us, event | category | flops | bytes accessed | tf_op | source)
XLA Modules:
  0.0 135.4 jit_solution(12694781207658293571)
XLA Ops:
  0.0 134.6 %shard_map.64 = bf16[128,1024]{1,0:T(8,128)(2,1)S(1)} custom-call(s32[8,128]{1,0:T(8,128)} %bitcast.8, f32[8,128]{1,0:T(8,128)} %bitcast.9, bf16[128,1024]{1,0:T(8,128)(2,1)} %tok_ref.1, bf16[1024,1536]{1,0:T(8,128)(2,1)} %bitcast.5, bf16[1024,1536]{1,0:T(8,128)(2,1)} %bitcast.6, bf16[1536,1024]{1,0:T(8,128)(2,1)} %bitcast.7), custom_call_target="tpu_custom_call" | custom-call | flops 12999999488 | bytes 10000000 | tf_op jit(solution)/shard_map/pallas_call | solution.py:389
  134.6 0.7 copy.8

commit v8 on v7

--- a/solution.py
+++ b/solution.py
@@ -21,16 +21,16 @@
 ORDER = tuple(
     tuple(divmod(unit, 10) for unit in chunk)
     for chunk in (
-        (0, 3),
-        (1, 10),
-        (13, 11, 21, 12),
-        (41, 60, 50, 51),
-        (70, 63, 71, 61),
-        (62, 53, 72, 73),
-        (52, 31, 42, 43),
-        (32, 40, 30, 33),
-        (23, 22),
+        (1, 0),
         (2, 20),
+        (23, 11, 21, 12),
+        (22, 31, 60, 41),
+        (70, 42, 62, 61),
+        (72, 63, 71, 73),
+        (51, 53, 43, 52),
+        (32, 40, 50, 33),
+        (13, 30),
+        (10, 3),
     )
 )
 CHUNKS, SMALL, LARGE = len(ORDER), 2, 4
@@ -43,20 +43,20 @@
 FIRST = ()
 ALL_STEPS = tuple(range(CHUNKS + 2))
 EARLY_A = (1, 2, 3, 4, 5, 6, 7, 8, 9, 10)
-EARLY_M = (0, 1, 2, 3, 5, 8, 9)
-EARLY_F = (1,)
+EARLY_M = (0, 1, 2, 3, 4, 5, 6, 8, 9)
+EARLY_F = (1, 3, 4, 5, 6)
 LATE_A = ()
-LATE_M = (4, 6, 7)
-LATE_F = (2, 3, 4, 5, 6, 7, 8, 9, 10)
-AFTER_P = {0: ((PLANE_IN, 1),), 6: ((SHARE, 3),), 7: ((SHARE, 7),), 8: ((COMBINE, 6),)}
-AFTER_EARLY_A = {2: ((PLANE_IN, 5),), 3: ((SHARE, 2), (PLANE_IN, 7)), 8: ((COMBINE, 7), (LEAVE, 6), (LEAVE, 7)), 9: ((COMBINE, 5), (LEAVE, 5)), 10: ((LEAVE, 4),)}
-AFTER_EARLY_M = {0: ((PLANE_IN, 2),), 1: ((PLANE_IN, 3), (PLANE_IN, 4)), 2: ((PLANE_IN, 6),), 5: ((SHARE, 1),)}
-AFTER_EARLY_F = {}
-AFTER_D = {10: ((COMBINE, 3), (LEAVE, 3))}
+LATE_M = (7,)
+LATE_F = (2, 7, 8, 9, 10)
+AFTER_P = {0: ((PLANE_IN, 1),), 2: ((SHARE, 3),)}
+AFTER_EARLY_A = {1: ((SHARE, 1), (SHARE, 2)), 5: ((SHARE, 6),), 8: ((COMBINE, 6), (LEAVE, 6), (COMBINE, 7), (LEAVE, 7)), 10: ((COMBINE, 4), (LEAVE, 4))}
+AFTER_EARLY_M = {0: ((PLANE_IN, 2),), 1: ((PLANE_IN, 3),), 2: ((PLANE_IN, 5), (PLANE_IN, 6)), 3: ((PLANE_IN, 7),), 4: ((SHARE, 7), (SHARE, 5))}
+AFTER_EARLY_F = {1: ((PLANE_IN, 4),)}
+AFTER_D = {}
 AFTER_A = {}
-AFTER_M = {4: ((SHARE, 5),), 7: ((SHARE, 4), (SHARE, 6), (SHARE, 0))}
-AFTER_F = {6: ((COMBINE, 1),), 9: ((COMBINE, 4),)}
-LAST = ((COMBINE, 2), (LEAVE, 2), (LEAVE, 1), (COMBINE, 0))
+AFTER_M = {}
+AFTER_F = {7: ((SHARE, 0),), 9: ((COMBINE, 5), (LEAVE, 5), (SHARE, 4)), 10: ((COMBINE, 3), (LEAVE, 3))}
+LAST = ((COMBINE, 2), (LEAVE, 2), (COMBINE, 1), (LEAVE, 1), (COMBINE, 0))
 
 def body(
     rt_ref, wt_ref, tok_ref, wg_ref, wu_ref, wd_ref, out_ref,
@@ -305,15 +305,19 @@
             rows = jnp.concatenate([first, first, last, last], axis=0)
             zp[p, :, cols] = jnp.dot(weights, rows, preferred_element_type=F32)
 
+    z_parts = [pl.ds(0, tok // 2), pl.ds(tok // 2, tok // 2)]
+
     def leave(p):
         out, base, to = (LEFT_OUT, 0, down_z) if p in LEFT_OUT else (RIGHT_OUT, len(LEFT_OUT), up_z)
         h = base + out.index(p)
-        total = zp[p]
-        if h > base:
-            arrived(zr.at[h - 1], z_rs.at[h - 1])
-            total = total + zr[h - 1].astype(F32)
-        zs[h] = total.astype(BF16)
-        remote(zs.at[h], zr.at[h], z_ss, z_rs.at[h], to).start()
+        for part, rows in enumerate(z_parts):
+            at = slice(rows.start, rows.start + rows.size)
+            total = zp[p, at]
+            if h > base:
+                arrived(zr.at[h - 1, rows], z_rs.at[h - 1, part])
+                total = total + zr[h - 1, at].astype(F32)
+            zs[h, at] = total.astype(BF16)
+            remote(zs.at[h, rows], zr.at[h, rows], z_ss, z_rs.at[h, part], to).start()
 
     ops = {PLANE_IN: z_arrived, COMBINE: combine, LEAVE: leave, SHARE: share}
 
@@ -362,9 +366,11 @@
     lax.fori_loop(0, CHUNKS + 2, step, 0)
     perform(LAST)
     last_left, last_right = len(LEFT_OUT) - 1, len(LEFT_OUT) + len(RIGHT_OUT) - 1
-    arrived(zr.at[last_right], z_rs.at[last_right])
-    arrived(zr.at[last_left], z_rs.at[last_left])
-    out_ref[...] = (zp[0] + zr[last_left].astype(F32) + zr[last_right].astype(F32)).astype(BF16)
+    for part, rows in enumerate(z_parts):
+        at = slice(rows.start, rows.start + rows.size)
+        arrived(zr.at[last_right, rows], z_rs.at[last_right, part])
+        arrived(zr.at[last_left, rows], z_rs.at[last_left, part])
+        out_ref[at] = (zp[0, at] + zr[last_left, at].astype(F32) + zr[last_right, at].astype(F32)).astype(BF16)
 
     sent(meta_all.at[pl.ds(1, NZ - 1)], zm_ss)
     sent(tok_all.at[pl.ds(1, NZ - 1)], zt_ss)
@@ -435,7 +441,7 @@
             dma,
             dma((NZ, NX)),
             dma,
-            dma((NZ - 1,)),
+            dma((NZ - 1, 2)),
         ],
         compiler_params=pltpu.CompilerParams(
             collective_id=0, has_side_effects=True, vmem_limit_bytes=60 * 1024 * 1024

time: 135 us -> 133 us (0.985)
  Pallas kernels: 135 us -> 132 us
    pallas_call x1, Pallas kernels: 135 us -> 132 us  [shards(): pl.pallas_call(body, out_shape=vm((tok, width), BF16), in_specs=[any_spac...]
where the time goes in v8:
time: 133 us
  Pallas kernels  132 us (99%)
    pallas_call x1, Pallas kernels, shards(): pl.pallas_call(body, out_shape=vm((tok, width), BF16), in_specs=[any_spac...  132 us

profile of v8, /device:TPU:1, one launch (start us, length us, event | category | flops | bytes accessed | tf_op | source)
XLA Modules:
  0.0 133.1 jit_solution(11818195523897226890)
XLA Ops:
  0.0 132.4 %shard_map.64 = bf16[128,1024]{1,0:T(8,128)(2,1)S(1)} custom-call(s32[8,128]{1,0:T(8,128)} %bitcast.8, f32[8,128]{1,0:T(8,128)} %bitcast.9, bf16[128,1024]{1,0:T(8,128)(2,1)} %tok_ref.1, bf16[1024,1536]{1,0:T(8,128)(2,1)} %bitcast.5, bf16[1024,1536]{1,0:T(8,128)(2,1)} %bitcast.6, bf16[1536,1024]{1,0:T(8,128)(2,1)} %bitcast.7), custom_call_target="tpu_custom_call" | custom-call | flops 12999999488 | bytes 10000000 | tf_op jit(solution)/shard_map/pallas_call | solution.py:395
  132.4 0.7 copy.8

commit v9 on v8

--- a/solution.py
+++ b/solution.py
@@ -106,16 +106,13 @@
         load.start()
 
     loads = []
-    for r in range(NY):
+    for r in (2, 1, 3, 0):
         cols = pl.ds(pl.multiple_of(lax.rem(y + r, NY) * fq, 128), fq)
         loads += [
             pltpu.make_async_copy(wg_ref.at[:, cols], wgu.at[:, pl.ds(2 * r * fq, fq)], w_sem.at[3 * r]),
             pltpu.make_async_copy(wu_ref.at[:, cols], wgu.at[:, pl.ds((2 * r + 1) * fq, fq)], w_sem.at[3 * r + 1]),
             pltpu.make_async_copy(wd_ref.at[cols], wdn.at[pl.ds(r * fq, fq)], w_sem.at[3 * r + 2]),
         ]
-    for load in loads:
-        load.start()
-
     place = lax.rem(lax.broadcasted_iota(jnp.int32, (PLANE * MAIN, tok), 0), MAIN)
     main_slot = place.astype(F32)
     tail_slot = [
@@ -244,7 +241,7 @@
 
     def half(i, n, r, h):
         low, high = parts(n)[h]
-        return hid.at[i, pl.ds(low, high - low), pl.ds(r * fq, fq)]
+        return hid.at[i, r, pl.ds(low, high - low)]
 
     def activate(i, n):
         for h, (low, high) in enumerate(parts(n)):
@@ -253,7 +250,7 @@
                 arrived(qr.at[d, i, at], q_rs.at[d, i, h])
             total = own[lax.rem(i, 2), rs] + qr[0, i, rs].astype(F32) + qr[1, i, rs].astype(F32)
             gate, up = total[:, :fq], total[:, fq:]
-            hid[i, rs, :fq] = (gate / (1.0 + jnp.exp(-gate)) * up).astype(BF16)
+            hid[i, 0, rs] = (gate / (1.0 + jnp.exp(-gate)) * up).astype(BF16)
             remote(half(i, n, 0, h), half(i, n, 3, h), ag_ss, ag_rs.at[0, i, h], up_y).start()
             remote(half(i, n, 0, h), half(i, n, 1, h), ag_ss, ag_rs.at[1, i, h], down_y).start()
 
@@ -280,7 +277,8 @@
         arrived(half(i, n, 2, 0), fw_rs.at[0, i])
         arrived(half(i, n, 2, 1), fw_rs.at[1, i])
         rows, whole = n * UNIT, n * UROWS
-        erow[:rows] = jnp.dot(hid[i, :rows], wdn[...], preferred_element_type=F32).astype(BF16)
+        hidden = jnp.concatenate([hid[i, r, :rows] for r in range(NY)], axis=1)
+        erow[:rows] = jnp.dot(hidden, wdn[...], preferred_element_type=F32).astype(BF16)
         eout[i, :whole, :width] = erow[:whole]
         tail = jnp.zeros((whole, block), F32)
         for b in range(CUT):
@@ -339,6 +337,8 @@
     pl.semaphore_wait(barrier, len(partners))
     z_send(0)
     dispatch(0)
+    for load in loads:
+        load.start()
     perform(FIRST)
     for load in loads:
         load.wait()
@@ -415,7 +415,7 @@
             vm((2, n, ROWS, 2 * fq), BF16),
             vm((2, n, ROWS, 2 * fq), BF16),
             vm((2, ROWS, 2 * fq), F32),
-            vm((n, ROWS, ff), BF16),
+            vm((n, NY, ROWS, fq), BF16),
             vm((ROWS, width), BF16),
             vm((n, LARGE * UROWS, wide), BF16),
             vm((NZ, PLANE * MAIN, wide), BF16),

time: 133 us -> 132 us (level)
  no operation moved by 1% of the time
where the time goes in v9:
time: 132 us
  Pallas kernels  131 us (99%)
    pallas_call x1, Pallas kernels, shards(): pl.pallas_call(body, out_shape=vm((tok, width), BF16), in_specs=[any_spac...  131 us

profile of v9, /device:TPU:1, one launch (start us, length us, event | category | flops | bytes accessed | tf_op | source)
XLA Modules:
  0.0 131.9 jit_solution(1763293987040361502)
XLA Ops:
  0.0 131.2 %shard_map.64 = bf16[128,1024]{1,0:T(8,128)(2,1)S(1)} custom-call(s32[8,128]{1,0:T(8,128)} %bitcast.8, f32[8,128]{1,0:T(8,128)} %bitcast.9, bf16[128,1024]{1,0:T(8,128)(2,1)} %tok_ref.1, bf16[1024,1536]{1,0:T(8,128)(2,1)} %bitcast.5, bf16[1024,1536]{1,0:T(8,128)(2,1)} %bitcast.6, bf16[1536,1024]{1,0:T(8,128)(2,1)} %bitcast.7), custom_call_target="tpu_custom_call" | custom-call | flops 12999999488 | bytes 10000000 | tf_op jit(solution)/shard_map/pallas_call | solution.py:395
  131.2 0.7 copy.8

commit v10 on v9

--- a/solution.py
+++ b/solution.py
@@ -21,16 +21,16 @@
 ORDER = tuple(
     tuple(divmod(unit, 10) for unit in chunk)
     for chunk in (
-        (1, 0),
-        (2, 20),
-        (23, 11, 21, 12),
-        (22, 31, 60, 41),
-        (70, 42, 62, 61),
-        (72, 63, 71, 73),
-        (51, 53, 43, 52),
-        (32, 40, 50, 33),
-        (13, 30),
-        (10, 3),
+        (3, 0),
+        (10, 20),
+        (21, 30, 12, 22),
+        (51, 41, 50, 60),
+        (70, 62, 71, 61),
+        (72, 73, 63, 52),
+        (31, 53, 42, 43),
+        (40, 32, 23, 33),
+        (13, 11),
+        (2, 1),
     )
 )
 CHUNKS, SMALL, LARGE = len(ORDER), 2, 4
@@ -44,19 +44,19 @@
 ALL_STEPS = tuple(range(CHUNKS + 2))
 EARLY_A = (1, 2, 3, 4, 5, 6, 7, 8, 9, 10)
 EARLY_M = (0, 1, 2, 3, 4, 5, 6, 8, 9)
-EARLY_F = (1, 3, 4, 5, 6)
+EARLY_F = (1, 2, 4, 5)
 LATE_A = ()
 LATE_M = (7,)
-LATE_F = (2, 7, 8, 9, 10)
-AFTER_P = {0: ((PLANE_IN, 1),), 2: ((SHARE, 3),)}
-AFTER_EARLY_A = {1: ((SHARE, 1), (SHARE, 2)), 5: ((SHARE, 6),), 8: ((COMBINE, 6), (LEAVE, 6), (COMBINE, 7), (LEAVE, 7)), 10: ((COMBINE, 4), (LEAVE, 4))}
-AFTER_EARLY_M = {0: ((PLANE_IN, 2),), 1: ((PLANE_IN, 3),), 2: ((PLANE_IN, 5), (PLANE_IN, 6)), 3: ((PLANE_IN, 7),), 4: ((SHARE, 7), (SHARE, 5))}
-AFTER_EARLY_F = {1: ((PLANE_IN, 4),)}
+LATE_F = (3, 6, 7, 8, 9, 10)
+AFTER_P = {0: ((PLANE_IN, 1), (SHARE, 1), (PLANE_IN, 2)), 7: ((SHARE, 7),), 8: ((SHARE, 5), (SHARE, 0), (COMBINE, 7), (COMBINE, 6), (LEAVE, 6))}
+AFTER_EARLY_A = {1: ((PLANE_IN, 3),), 2: ((PLANE_IN, 5),), 3: ((PLANE_IN, 7), (SHARE, 4)), 8: ((LEAVE, 7),), 10: ((LEAVE, 4),)}
+AFTER_EARLY_M = {1: ((SHARE, 3), (PLANE_IN, 4), (SHARE, 2)), 2: ((PLANE_IN, 6),)}
+AFTER_EARLY_F = {}
 AFTER_D = {}
 AFTER_A = {}
 AFTER_M = {}
-AFTER_F = {7: ((SHARE, 0),), 9: ((COMBINE, 5), (LEAVE, 5), (SHARE, 4)), 10: ((COMBINE, 3), (LEAVE, 3))}
-LAST = ((COMBINE, 2), (LEAVE, 2), (COMBINE, 1), (LEAVE, 1), (COMBINE, 0))
+AFTER_F = {6: ((SHARE, 6),), 9: ((COMBINE, 5), (LEAVE, 5), (COMBINE, 4)), 10: ((COMBINE, 2), (COMBINE, 3), (LEAVE, 3))}
+LAST = ((COMBINE, 1), (LEAVE, 2), (LEAVE, 1), (COMBINE, 0))
 
 def body(
     rt_ref, wt_ref, tok_ref, wg_ref, wu_ref, wd_ref, out_ref,
@@ -105,14 +105,15 @@
     for load in inputs:
         load.start()
 
-    loads = []
+    gate_up, to_width = {}, []
     for r in (2, 1, 3, 0):
         cols = pl.ds(pl.multiple_of(lax.rem(y + r, NY) * fq, 128), fq)
-        loads += [
+        gate_up[r] = [
             pltpu.make_async_copy(wg_ref.at[:, cols], wgu.at[:, pl.ds(2 * r * fq, fq)], w_sem.at[3 * r]),
             pltpu.make_async_copy(wu_ref.at[:, cols], wgu.at[:, pl.ds((2 * r + 1) * fq, fq)], w_sem.at[3 * r + 1]),
-            pltpu.make_async_copy(wd_ref.at[cols], wdn.at[pl.ds(r * fq, fq)], w_sem.at[3 * r + 2]),
         ]
+        to_width.append(pltpu.make_async_copy(wd_ref.at[cols], wdn.at[pl.ds(r * fq, fq)], w_sem.at[3 * r + 2]))
+
     place = lax.rem(lax.broadcasted_iota(jnp.int32, (PLANE * MAIN, tok), 0), MAIN)
     main_slot = place.astype(F32)
     tail_slot = [
@@ -213,6 +214,13 @@
             xrows[whole:rows, b * block : (b + 1) * block] = tail.astype(BF16)
 
         def part(r):
+            if len(ORDER[0]) == n:
+
+                @pl.when(i == 0)
+                def _():
+                    for load in gate_up[r]:
+                        load.wait()
+
             return jnp.dot(xrows[:rows], wgu[:, 2 * r * fq : 2 * (r + 1) * fq], preferred_element_type=F32)
 
         far = part(2)
@@ -277,6 +285,13 @@
         arrived(half(i, n, 2, 0), fw_rs.at[0, i])
         arrived(half(i, n, 2, 1), fw_rs.at[1, i])
         rows, whole = n * UNIT, n * UROWS
+        if len(ORDER[0]) == n:
+
+            @pl.when(i == 0)
+            def _():
+                for load in to_width:
+                    load.wait()
+
         hidden = jnp.concatenate([hid[i, r, :rows] for r in range(NY)], axis=1)
         erow[:rows] = jnp.dot(hidden, wdn[...], preferred_element_type=F32).astype(BF16)
         eout[i, :whole, :width] = erow[:whole]
@@ -337,11 +352,9 @@
     pl.semaphore_wait(barrier, len(partners))
     z_send(0)
     dispatch(0)
-    for load in loads:
+    for load in [*gate_up[2], *gate_up[1], *gate_up[3], *gate_up[0], *to_width]:
         load.start()
     perform(FIRST)
-    for load in loads:
-        load.wait()
 
     def step(s, carry):
         for run, lag, steps, table in (

time: 132 us -> 133 us (level)
  no operation moved by 1% of the time
where the time goes in v10:
time: 133 us
  Pallas kernels  132 us (99%)
    pallas_call x1, Pallas kernels, shards(): pl.pallas_call(body, out_shape=vm((tok, width), BF16), in_specs=[any_spac...  132 us

profile of v10, /device:TPU:1, one launch (start us, length us, event | category | flops | bytes accessed | tf_op | source)
XLA Modules:
  0.0 132.8 jit_solution(17169976468433281007)
XLA Ops:
  0.0 132.1 %shard_map.64 = bf16[128,1024]{1,0:T(8,128)(2,1)S(1)} custom-call(s32[8,128]{1,0:T(8,128)} %bitcast.8, f32[8,128]{1,0:T(8,128)} %bitcast.9, bf16[128,1024]{1,0:T(8,128)(2,1)} %tok_ref.1, bf16[1024,1536]{1,0:T(8,128)(2,1)} %bitcast.5, bf16[1024,1536]{1,0:T(8,128)(2,1)} %bitcast.6, bf16[1536,1024]{1,0:T(8,128)(2,1)} %bitcast.7), custom_call_target="tpu_custom_call" | custom-call | flops 12999999488 | bytes 10000000 | tf_op jit(solution)/shard_map/pallas_call | solution.py:408
  132.1 0.7 copy.8

commit v11 on v9

--- a/solution.py
+++ b/solution.py
@@ -105,14 +105,15 @@
     for load in inputs:
         load.start()
 
-    loads = []
+    gate_up, to_width = {}, []
     for r in (2, 1, 3, 0):
         cols = pl.ds(pl.multiple_of(lax.rem(y + r, NY) * fq, 128), fq)
-        loads += [
+        gate_up[r] = [
             pltpu.make_async_copy(wg_ref.at[:, cols], wgu.at[:, pl.ds(2 * r * fq, fq)], w_sem.at[3 * r]),
             pltpu.make_async_copy(wu_ref.at[:, cols], wgu.at[:, pl.ds((2 * r + 1) * fq, fq)], w_sem.at[3 * r + 1]),
-            pltpu.make_async_copy(wd_ref.at[cols], wdn.at[pl.ds(r * fq, fq)], w_sem.at[3 * r + 2]),
         ]
+        to_width.append(pltpu.make_async_copy(wd_ref.at[cols], wdn.at[pl.ds(r * fq, fq)], w_sem.at[3 * r + 2]))
+
     place = lax.rem(lax.broadcasted_iota(jnp.int32, (PLANE * MAIN, tok), 0), MAIN)
     main_slot = place.astype(F32)
     tail_slot = [
@@ -213,6 +214,13 @@
             xrows[whole:rows, b * block : (b + 1) * block] = tail.astype(BF16)
 
         def part(r):
+            if len(ORDER[0]) == n:
+
+                @pl.when(i == 0)
+                def _():
+                    for load in gate_up[r]:
+                        load.wait()
+
             return jnp.dot(xrows[:rows], wgu[:, 2 * r * fq : 2 * (r + 1) * fq], preferred_element_type=F32)
 
         far = part(2)
@@ -277,6 +285,13 @@
         arrived(half(i, n, 2, 0), fw_rs.at[0, i])
         arrived(half(i, n, 2, 1), fw_rs.at[1, i])
         rows, whole = n * UNIT, n * UROWS
+        if len(ORDER[0]) == n:
+
+            @pl.when(i == 0)
+            def _():
+                for load in to_width:
+                    load.wait()
+
         hidden = jnp.concatenate([hid[i, r, :rows] for r in range(NY)], axis=1)
         erow[:rows] = jnp.dot(hidden, wdn[...], preferred_element_type=F32).astype(BF16)
         eout[i, :whole, :width] = erow[:whole]
@@ -337,11 +352,9 @@
     pl.semaphore_wait(barrier, len(partners))
     z_send(0)
     dispatch(0)
-    for load in loads:
+    for load in [*gate_up[2], *gate_up[1], *gate_up[3], *gate_up[0], *to_width]:
         load.start()
     perform(FIRST)
-    for load in loads:
-        load.wait()
 
     def step(s, carry):
         for run, lag, steps, table in (

time: 132 us -> 132 us (level)
  no operation moved by 1% of the time
where the time goes in v11:
time: 132 us
  Pallas kernels  131 us (99%)
    pallas_call x1, Pallas kernels, shards(): pl.pallas_call(body, out_shape=vm((tok, width), BF16), in_specs=[any_spac...  131 us

profile of v11, /device:TPU:1, one launch (start us, length us, event | category | flops | bytes accessed | tf_op | source)
XLA Modules:
  0.0 131.9 jit_solution(6647515670398056973)
XLA Ops:
  0.0 131.2 %shard_map.64 = bf16[128,1024]{1,0:T(8,128)(2,1)S(1)} custom-call(s32[8,128]{1,0:T(8,128)} %bitcast.8, f32[8,128]{1,0:T(8,128)} %bitcast.9, bf16[128,1024]{1,0:T(8,128)(2,1)} %tok_ref.1, bf16[1024,1536]{1,0:T(8,128)(2,1)} %bitcast.5, bf16[1024,1536]{1,0:T(8,128)(2,1)} %bitcast.6, bf16[1536,1024]{1,0:T(8,128)(2,1)} %bitcast.7), custom_call_target="tpu_custom_call" | custom-call | flops 12999999488 | bytes 10000000 | tf_op jit(solution)/shard_map/pallas_call | solution.py:408
  131.2 0.7 copy.8
